TPU v7x, 32 devices: a whole 2x2x4 slice. The times are simulated.
32 devices in a mesh: seq: 16 (over z, x, core), head: 2 (over y).
Axes of the slice: x: 2, y: 2, z: 4, core: 2. Of those that a mesh axis runs over, the one named last changes fastest.
Arguments:
- tokens: bfloat16 [4096, 768], P(('seq', 'head')), may hold values from -6 to 6
- cotangent: bfloat16 [4096, 768], P(('seq', 'head')), may hold values from -6 to 6
- w_query: bfloat16 [768, 768], P(('seq', 'head')), may hold values from -0.21875 to 0.21875
- w_key: bfloat16 [768, 768], P(('seq', 'head')), may hold values from -0.21875 to 0.21875
- w_value: bfloat16 [768, 768], P(('seq', 'head')), may hold values from -0.21875 to 0.21875
- w_output: bfloat16 [768, 768], P(('seq', 'head')), may hold values from -1.75 to 1.75
- w_inner: bfloat16 [768, 3072], P(('seq', 'head')), may hold values from -0.21875 to 0.21875
- w_outer: bfloat16 [3072, 768], P(('seq', 'head')), may hold values from -0.109375 to 0.109375
- gain_first: float32 [768], replicated, may hold values from 0.1 to 1.9
- shift_first: float32 [768], replicated, may hold values from -1.5 to 1.5
- gain_second: float32 [768], replicated, may hold values from 0.1 to 1.9
- shift_second: float32 [768], replicated, may hold values from -1.5 to 1.5
- attn_down: bfloat16 [8, 4, 16, 768], replicated, may hold values from -0.21875 to 0.21875
- attn_up: bfloat16 [8, 4, 16, 768], replicated, may hold values from -1 to 1
- inner_down: bfloat16 [8, 16, 768], replicated, may hold values from -0.21875 to 0.21875
- inner_up: bfloat16 [8, 16, 3072], replicated, may hold values from -1 to 1
- outer_down: bfloat16 [8, 16, 3072], replicated, may hold values from -0.109375 to 0.109375
- outer_up: bfloat16 [8, 16, 768], replicated, may hold values from -1 to 1
- lengths: int32 [1], replicated, may hold values from 1024 to 4096, as said below
- rand_blocks: int32 [64, 3], P('seq'), may hold values from 2 to 63, as said below
- adapter_pick: int32 [1], replicated, may hold values from 0 to 7
Outputs:
- output: bfloat16 [4096, 768], P(('seq', 'head'))
- grad_tokens: float32 [4096, 768], P(('seq', 'head'))
- grad_attn_down: float32 [8, 4, 16, 768], replicated
- grad_attn_up: float32 [8, 4, 16, 768], replicated
- grad_inner_down: float32 [8, 16, 768], replicated
- grad_inner_up: float32 [8, 16, 3072], replicated
- grad_outer_down: float32 [8, 16, 3072], replicated
- grad_outer_up: float32 [8, 16, 768], replicated
Inputs may be any that keep to these rules, and one draw needn't show every extreme that they name: `lengths`: one sequence, drawn from the seed, has at least 3968 used slots. `rand_blocks`: row b names three different blocks of its own sequence, none of them 0, 1, b - 1, b or b + 1.
All inputs are finite; a program needn't handle non-finite values.
Results may differ from a plain program's by a relative error of at most 0.018.
The roundings to bfloat16 on the way count: a program that leaves them out, or rounds other values in their place, can miss the bound.
Values may be sent and summed in bfloat16 or wider, within the bound.
No kernel may reach another device: no remote copies, remote signals or barrier semaphores. Data moves between devices by JAX's collectives and lax.ppermute only.
A program may use at most 640 MiB of HBM per device.

v0:
```python
import functools

import jax
import jax.numpy as jnp
from jax import lax
from jax.experimental import pallas as pl
from jax.experimental.pallas import tpu as pltpu
from jax.sharding import PartitionSpec as P

D = 768
HEADS = 12
HDIM = 64
BLOCK = 64
ADAPTERS = 8
RANK = 16
FF = 3072

PEERS = (0, 8, 16, 24)
PLANE = (0, 1, 4, 5)
GROUP_HEADS = HEADS // 4
SHARE = GROUP_HEADS * HDIM
WIDE = 256
LSE_LANE = SHARE
DEL_LANE = SHARE + 9
MASK_LANE = SHARE + 18
FLOOR = -1e30
STACK = GROUP_HEADS * BLOCK
AXES = ("seq", "head")
norm_eps = 1e-12
f32 = jnp.float32
bf16 = jnp.bfloat16
VMEM_LIMIT = 60 * 1024 * 1024


def dense_mul(left_op, right_op):
    return jnp.dot(left_op, right_op, preferred_element_type=f32)


def dense_right_t(left_op, right_op):
    return lax.dot_general(left_op, right_op, (((1,), (1,)), ((), ())), preferred_element_type=f32)


def dense_left_t(left_op, right_op):
    return lax.dot_general(left_op, right_op, (((0,), (0,)), ((), ())), preferred_element_type=f32)


def lanes(rows):
    return lax.broadcasted_iota(jnp.int32, (rows, WIDE), 1)


def head_lanes(lane, head):
    return (lane >= HDIM * head) & (lane < HDIM * (head + 1))


def part_lanes(lane, first, head):
    return (lane >= first + 3 * head) & (lane < first + 3 * head + 3)


def project_rows(raw, u_ref):
    lane = lanes(raw.shape[0])
    data = lane < SHARE

    def part(j):
        piece = raw[:, WIDE * j : WIDE * (j + 1)]
        return (piece + dense_mul(piece[:, WIDE // 2 :].astype(bf16), u_ref[j])).astype(bf16).astype(f32)

    query = jnp.where(data, part(0) * 0.125, jnp.where(lane == MASK_LANE, 1.0, 0.0)).astype(bf16)
    return query, jnp.concatenate([part(1)[:, :SHARE], part(2)[:, :SHARE]], axis=1).astype(bf16)


def widen_pair(pair, position, seq_length):
    lane = lanes(pair.shape[0])
    data = lane < SHARE
    blank = jnp.zeros((pair.shape[0], WIDE - SHARE), bf16)
    key = jnp.concatenate([pair[:, :SHARE], blank], axis=1)
    value = jnp.concatenate([pair[:, SHARE:], blank], axis=1)
    mask = jnp.where(position < seq_length, 0.0, FLOOR)
    key_side = jnp.where(lane < DEL_LANE, 1.0, jnp.where(lane == MASK_LANE, mask, 0.0)).astype(bf16)
    value_side = jnp.where((lane >= DEL_LANE) & (lane < MASK_LANE), 1.0, 0.0).astype(bf16)
    return jnp.where(data, key, key_side), jnp.where(data, value, value_side)


def slab_offset(n, place, fast):
    if not fast:
        return (n & 7) | ((n >> 3) << 5)
    core = (place >> 1) & 1
    near = 4 - 3 * core if n < 4 else 1 + 3 * core
    return (0, near, 5 - near, 5)[n % 4] ^ (2 * (n // 4))


def slab_row(offset):
    return (offset & 7) | ((offset >> 5) << 3)


def plane_quarter(place):
    return (place & 1) | ((place >> 1) & 2)


def rand_at(fast, rand_ref, block, r):
    if not fast:
        return rand_ref[block * 3 + r]
    return rand_ref[(block // 4) * 2, WIDE // 4 + (block & 3) * 3 + r]


def pack_kernel(rand_ref, query_ref, key_ref, value_ref, output_ref, inner_ref, outer_ref, late_ref, *slice_refs):
    slab = query_ref.shape[0]
    group = ((lax.axis_index("seq") * lax.axis_size("head") + lax.axis_index("head")) >> 3) & 3
    late_ref[:, :D] = output_ref[...]
    late_ref[:, D : D + FF] = inner_ref[...]
    outer = outer_ref[...].astype(f32)
    for c in range(FF // D):
        late_ref[:, D + FF + D * c : D + FF + D * (c + 1)] = outer[slab * c : slab * (c + 1)].astype(bf16)
    spare = (slab, WIDE - SHARE)
    lane = lax.broadcasted_iota(jnp.int32, spare, 1)
    marks = jnp.zeros(spare, f32)
    for n in range(12):
        marks = jnp.where(lane == n, rand_ref[n // 3, n % 3].astype(f32), marks)
    marks = jnp.where(lax.broadcasted_iota(jnp.int32, spare, 0) == 0, marks, 0.0)
    sources = [ref[...].astype(f32) for ref in (query_ref, key_ref, value_ref)]
    for p in range(4):
        pieces = []
        for source in sources:
            mine = source[:, :SHARE]
            for g in range(1, 4):
                mine = jnp.where((group ^ p) == g, source[:, SHARE * g : SHARE * (g + 1)], mine)
            pieces += [mine, marks]
        slice_refs[p][...] = jnp.concatenate(pieces, axis=1).astype(bf16)


def put_tokens(fast, token_refs, tok_ref):
    rows = 2 * BLOCK
    if fast:
        own, far, near = token_refs
        parts = [own[...], near[:rows, :], far[...], near[rows:, :]]
    else:
        parts = [ref[...] for ref in token_refs]
    for a in range(4):
        tok_ref[rows * a : rows * (a + 1), :] = parts[a]


def project_kernel(fast, meta_ref, down_ref, up_ref, *refs):
    count = 3 if fast else 4
    tok_refs, refs = refs[:count], refs[count:]
    w_refs, (w_ref, down_stack_ref, up_stack_ref, q_ref, pair_ref, rand_ref, u_ref, tok_ref, wide_ref) = refs[:-9], refs[-9:]
    place = meta_ref[0]
    group = meta_ref[2]
    chosen = meta_ref[3]
    half = WIDE // 2
    lead = WIDE // 4
    rand_ref[...] = jnp.zeros_like(rand_ref)
    if fast:
        slab = D // 32
        for n, piece in enumerate(w_refs):
            rows = piece[...].astype(f32)
            for a in range(4):
                device = place ^ slab_offset(n, place, fast) ^ PEERS[a]
                wide_ref[pl.ds(pl.multiple_of(device * slab, 8), slab), :] = rows[slab * a : slab * (a + 1)]
                rand_ref[pl.ds(device, 1), :] = rows[slab * a : slab * a + 1, half:WIDE].astype(jnp.int32)
    else:
        wide_ref[...] = w_refs[0][...].astype(f32)
    own = lax.broadcasted_iota(jnp.int32, (D, half), 1) < lead
    above = jnp.zeros((lead, D), f32)
    below = jnp.zeros((half - lead - RANK, D), f32)
    side = jnp.zeros((RANK, WIDE - SHARE), f32)
    downs = []
    ups = []
    for j in range(3):
        low = slice(WIDE * j, WIDE * j + half)
        high = slice(WIDE * j + half, WIDE * (j + 1))
        turned = jnp.concatenate([above, down_ref[chosen, j].astype(f32), below], axis=0).T
        w_ref[:, low] = wide_ref[:, low].astype(bf16)
        w_ref[:, high] = jnp.where(own, wide_ref[:, high], turned).astype(bf16)
        up = up_ref[chosen, j].astype(f32)
        mine = jnp.zeros((RANK, SHARE), f32)
        for g in range(4):
            mine = mine + jnp.where(group == g, up[:, SHARE * g : SHARE * (g + 1)], 0.0)
        mine = jnp.concatenate([mine, side], axis=1)
        u_ref[j] = jnp.concatenate([above[:, :WIDE], mine, below[:, :WIDE]], axis=0).astype(bf16)
        downs.append(down_ref[chosen, j].astype(f32))
        ups.append(jnp.concatenate([mine if n == j else jnp.zeros_like(mine) for n in range(3)], axis=1))
    rest = jnp.zeros((half - 3 * RANK, D), f32)
    down_stack_ref[...] = jnp.concatenate(downs + [rest], axis=0).astype(bf16)
    up_stack_ref[...] = jnp.concatenate(ups + [rest], axis=0).astype(bf16)
    put_tokens(fast, tok_refs, tok_ref)
    q_ref[...], pair_ref[...] = project_rows(dense_mul(tok_ref[...], w_ref[...]), u_ref)


def block_rows(ref, block, count=1):
    return ref[pl.ds(pl.multiple_of(block * BLOCK, BLOCK), count * BLOCK), :]


def merge_heads(stacked):
    lane = lanes(BLOCK)
    total = jnp.zeros((BLOCK, WIDE), f32)
    for head in range(GROUP_HEADS):
        total = jnp.where(head_lanes(lane, head), stacked[BLOCK * head : BLOCK * (head + 1)], total)
    return total


def key_set(ref, picks, block, block_total, fill):
    own = block_rows(ref, block)
    left = block_rows(ref, jnp.maximum(block - 1, 0))
    right = block_rows(ref, jnp.minimum(block + 1, block_total - 1))
    if fill:
        blank = jnp.where(lanes(BLOCK) == MASK_LANE, FLOOR, 0.0).astype(bf16)
        left = jnp.where(block - 1 >= 2, left, blank)
        right = jnp.where(block + 1 < block_total, right, blank)
    rand = [block_rows(ref, pick) for pick in picks]
    return jnp.concatenate([own, left, right, block_rows(ref, 0, 2)] + rand, axis=0)


def own_block(place, t):
    return 2 * (place ^ PEERS[t // 2]) + t % 2


def attend_kernel(fast, meta_ref, rand_ref, q_ref, *refs):
    slab_refs, (k_ref, v_ref, *ctx_refs, aux_ref, s_ref) = refs[:-8], refs[-8:]
    place = meta_ref[0]
    piece = 2 * BLOCK
    for n, slab_ref in enumerate(slab_refs):
        for a in range(4):
            device = place ^ slab_offset(n, place, fast) ^ PEERS[a]
            here = pl.ds(pl.multiple_of(device * piece, piece), piece)
            position = device * piece + lax.broadcasted_iota(jnp.int32, (piece, WIDE), 0)
            k_ref[here, :], v_ref[here, :] = widen_pair(
                slab_ref[piece * a : piece * (a + 1), :], position, meta_ref[1]
            )
    total_rows = k_ref.shape[0]
    block_total = total_rows // BLOCK
    chunks = total_rows // (8 * BLOCK)

    def queries(t):
        rows = q_ref[pl.ds(t * BLOCK, BLOCK), :]
        lane = lanes(BLOCK)
        blank = jnp.zeros_like(rows)
        return jnp.concatenate(
            [
                jnp.where(head_lanes(lane, head) | (lane == MASK_LANE), rows, blank)
                for head in range(GROUP_HEADS)
            ],
            axis=0,
        )

    def finish(t, low, exact, top, total):
        lane = lanes(BLOCK)
        rows = pl.ds(t * BLOCK, BLOCK)
        ctx_refs[t // 2][pl.ds((t % 2) * BLOCK, BLOCK), :] = merge_heads(low).astype(bf16)
        aux = merge_heads(exact)
        lse = top + jnp.log(total)
        for head in range(GROUP_HEADS):
            aux = jnp.where(lane == LSE_LANE + head, lse[BLOCK * head : BLOCK * (head + 1)], aux)
        aux_ref[rows, :] = aux

    def split(probs):
        low = probs.astype(bf16)
        return low, (probs - low.astype(f32)).astype(bf16)

    def sparse(t):
        block = own_block(place, t)
        picks = [rand_at(fast, rand_ref, block, r) for r in range(3)]
        scores = dense_right_t(queries(t), key_set(k_ref, picks, block, block_total, True))
        top = jnp.max(scores, axis=1, keepdims=True)
        weights = jnp.exp(scores - top)
        total = jnp.sum(weights, axis=1, keepdims=True)
        low, rest = split(weights * (1.0 / total))
        values = key_set(v_ref, picks, block, block_total, False)
        context = dense_mul(low, values)
        return context, context + dense_mul(rest, values), top, total

    for a in range(4):

        @pl.when((place ^ PEERS[a]) != 0)
        def _(a=a):
            results = [sparse(2 * a), sparse(2 * a + 1)]
            finish(2 * a, *results[0])
            finish(2 * a + 1, *results[1])

    at_once = s_ref.shape[1] // STACK

    def full(a, first):
        stack = jnp.concatenate([queries(2 * a + first + n) for n in range(at_once)], axis=0)
        height = at_once * STACK

        def score(c, state):
            top, total, tops = state
            part = dense_right_t(stack, block_rows(k_ref, c * 8, 8))
            here = jnp.max(part, axis=1, keepdims=True)
            weights = jnp.exp(part - here)
            s_ref[c] = weights
            later = jnp.maximum(top, here)
            total = total * jnp.exp(top - later) + jnp.sum(weights, axis=1, keepdims=True) * jnp.exp(here - later)
            return later, total, jnp.where(turn == c, here, tops)

        turn = lax.broadcasted_iota(jnp.int32, (height, 128), 1)
        top, total, tops = lax.fori_loop(
            0,
            chunks,
            score,
            (jnp.full((height, 1), FLOOR, f32), jnp.zeros((height, 1), f32), jnp.full((height, 128), FLOOR, f32)),
        )
        scales = jnp.exp(tops - top) * (1.0 / total)

        def mix(c, state):
            scale = jnp.sum(jnp.where(turn == c, scales, 0.0), axis=1, keepdims=True)
            low, rest = split(s_ref[c] * scale)
            values = block_rows(v_ref, c * 8, 8)
            return (state[0] + dense_mul(low, values), state[1] + dense_mul(rest, values))

        zero = jnp.zeros((height, WIDE), f32)
        context, rest = lax.fori_loop(0, chunks, mix, (zero, zero), unroll=4)
        for n in range(at_once):
            here = slice(STACK * n, STACK * (n + 1))
            finish(2 * a + first + n, context[here], (context + rest)[here], top[here], total[here])

    for a in range(4):

        @pl.when((place ^ PEERS[a]) == 0)
        def _(a=a):
            for first in range(0, 2, at_once):
                full(a, first)


DENSE_ROWS = 96


def fold_rows(rows):
    last = rows[DENSE_ROWS:]
    beside = jnp.concatenate([last[:, HDIM * h : HDIM * (h + 1)] for h in range(GROUP_HEADS)], axis=0)
    return jnp.concatenate([rows[:DENSE_ROWS], beside], axis=1)


def unfold_rows(folded):
    beside = folded[:, SHARE:]
    count = DENSE_ROWS // GROUP_HEADS
    last = jnp.concatenate([beside[count * h : count * (h + 1)] for h in range(GROUP_HEADS)], axis=1)
    rows = jnp.concatenate([folded[:, :SHARE], last], axis=0)
    return jnp.concatenate([rows, jnp.zeros((rows.shape[0], WIDE - SHARE), rows.dtype)], axis=1)


def split_parts(value):
    high = value.astype(bf16).astype(f32)
    middle = (value - high).astype(bf16).astype(f32)
    return (high, middle, value - high - middle)


def delta_kernel(*refs):
    grad_refs, aux_ref, out_ref = refs[:4], refs[4], refs[5]
    rows = 2 * BLOCK
    lane = lanes(rows)
    for a in range(4):
        here = pl.ds(a * rows, rows)
        grad = unfold_rows(grad_refs[a][...]).astype(f32)
        aux = aux_ref[here, :]
        result = jnp.where(lane < SHARE, grad, 0.0)
        product = grad * aux
        for head in range(GROUP_HEADS):
            delta = jnp.sum(jnp.where(head_lanes(lane, head), product, 0.0), axis=1, keepdims=True)
            lse = jnp.sum(jnp.where(lane == LSE_LANE + head, aux, 0.0), axis=1, keepdims=True)
            for p, value in enumerate(split_parts(lse)):
                result = jnp.where(lane == LSE_LANE + 3 * head + p, -value, result)
            for p, value in enumerate(split_parts(delta)):
                result = jnp.where(lane == DEL_LANE + 3 * head + p, -value, result)
        out_ref[here, :] = result.astype(bf16)


def query_stacks(rows, grads):
    lane = lanes(BLOCK)
    blank = jnp.zeros_like(rows)
    queries = []
    outers = []
    for head in range(GROUP_HEADS):
        here = head_lanes(lane, head)
        queries.append(
            jnp.where(
                here | (lane == MASK_LANE), rows, jnp.where(part_lanes(lane, LSE_LANE, head), grads, blank)
            )
        )
        outers.append(jnp.where(here | part_lanes(lane, DEL_LANE, head), grads, blank))
    return jnp.concatenate(queries, axis=0), jnp.concatenate(outers, axis=0)


def near_kernel(fast, meta_ref, rand_ref, q_ref, k_ref, v_ref, g_ref, dq_ref, *refs):
    zero_outs, (blank_ref, sems) = refs[:-2], refs[-2:]
    place = meta_ref[0]
    block_total = k_ref.shape[0] // BLOCK
    copies = []
    if zero_outs:
        blank_ref[...] = jnp.zeros_like(blank_ref)
        for n, where in enumerate(zero_outs):
            shape = where.shape
            source = blank_ref if len(shape) == 4 else blank_ref.at[0 : shape[2] // D]
            for adapter in range(ADAPTERS):
                if len(shape) == 4:
                    copies.append((blank_ref, where.at[adapter], n))
                else:
                    for c in range(shape[2] // D):
                        copies.append((blank_ref.at[c], where.at[adapter, :, pl.ds(D * c, D)], n))
        copies = [pltpu.make_async_copy(source, where, sems.at[n]) for n, (source, where, _) in enumerate(copies)]
        for copy in copies:
            copy.start()

    def query_side(stack, outer, keys, values):
        probs = jnp.exp(dense_right_t(stack, keys))
        scored = (probs * dense_right_t(outer, values)).astype(bf16)
        return dense_mul(scored, keys)

    def place_of(a, k):
        return pl.ds(pl.multiple_of((2 * a + k) * BLOCK, BLOCK), BLOCK)

    def put_query(a, k, stacked):
        dq_ref[place_of(a, k), :] = (merge_heads(stacked) * 0.125).astype(bf16)

    def stacks(a, k):
        here = place_of(a, k)
        return query_stacks(q_ref[here, :], g_ref[here, :])

    def sparse(a, k):
        block = 2 * (place ^ (8 * a)) + k
        picks = [rand_at(fast, rand_ref, block, r) for r in range(3)]
        return query_side(
            *stacks(a, k),
            key_set(k_ref, picks, block, block_total, True),
            key_set(v_ref, picks, block, block_total, False),
        )

    def piece(a, carry):
        @pl.when((place ^ (8 * a)) != 0)
        def _():
            results = [sparse(a, 0), sparse(a, 1)]
            put_query(a, 0, results[0])
            put_query(a, 1, results[1])

        @pl.when((place ^ (8 * a)) == 0)
        def _():
            pairs = [stacks(a, 0), stacks(a, 1)]
            stack = jnp.concatenate([pair[0] for pair in pairs], axis=0)
            outer = jnp.concatenate([pair[1] for pair in pairs], axis=0)

            def add(c, total):
                return total + query_side(stack, outer, block_rows(k_ref, c * 8, 8), block_rows(v_ref, c * 8, 8))

            total = lax.fori_loop(0, block_total // 8, add, jnp.zeros((2 * STACK, WIDE), f32), unroll=2)
            put_query(a, 0, total[:STACK])
            put_query(a, 1, total[STACK:])

        return carry

    lax.fori_loop(0, 4, piece, 0)
    for copy in copies:
        copy.wait()


def collect_kernel(fast, block_total, meta_ref, rand_ref, pair_ref):
    place = meta_ref[0]

    def collect(block, count):
        for r in range(3):
            target = rand_at(fast, rand_ref, block, r)
            mine = (((target // 2) ^ place) & ~24) == 0

            @pl.when(mine)
            def _(target=target, count=count):
                pair_ref[count + 1] = target * 65536 + block

            count = count + mine.astype(jnp.int32)
        return count

    pair_ref[0] = lax.fori_loop(2, block_total, collect, jnp.int32(0))


def far_kernel(fast, meta_ref, pair_ref, k_ref, v_ref, dq_ref, w_ref, down_ref, up_ref, early_ref, *refs):
    count = 3 if fast else 4
    tok_refs, refs = refs[:count], refs[count:]
    slab_refs, refs = refs[:-11], refs[-11:]
    part_refs, near_ref, away_ref, refs = refs[:2], refs[2], refs[3], refs[4:]
    q_ref, g_ref, dk_ref, dv_ref, grad_ref, tok_ref, terms_ref = refs
    place = meta_ref[0]
    group = meta_ref[2]
    block_total = k_ref.shape[0] // BLOCK
    count = len(slab_refs) // 2
    rows = 2 * BLOCK
    for n in range(count):
        here = pl.ds(pl.multiple_of(slab_row(slab_offset(n, place, fast)) * 4 * rows, rows), 4 * rows)
        q_ref[here, :] = slab_refs[n][...]
        g_ref[here, :] = slab_refs[count + n][...]

    def stacks(blocks):
        pairs = []
        for block in blocks:
            other = (block // 2) ^ place
            where = slab_row(other) * 8 + ((other >> 3) & 3) * 2 + (block & 1)
            pairs.append(query_stacks(block_rows(q_ref, where), block_rows(g_ref, where)))
        return (
            jnp.concatenate([pair[0] for pair in pairs], axis=0),
            jnp.concatenate([pair[1] for pair in pairs], axis=0),
        )

    def key_side(keys, values, blocks, allowed):
        stack, outer = stacks(blocks)
        probs = jnp.exp(dense_right_t(keys, stack))
        if allowed is not None:
            probs = jnp.where(allowed, probs, 0.0)
        scored = (probs * dense_right_t(values, outer)).astype(bf16)
        return dense_mul(scored, stack), dense_mul(probs.astype(bf16), outer)

    def put(here, grads):
        dk_ref[here, :] += grads[0]
        dv_ref[here, :] += grads[1]

    key_local = lax.broadcasted_iota(jnp.int32, (rows, 6 * STACK), 0) // BLOCK
    turn = lax.broadcasted_iota(jnp.int32, (rows, 6 * STACK), 1) // STACK
    for a in range(4):
        first = 2 * (place ^ PEERS[a])
        here = slice(rows * a, rows * (a + 1))
        blocks = [0, 1, jnp.maximum(first - 1, 0), first, first + 1, jnp.minimum(first + 2, block_total - 1)]
        key_block = first + key_local
        block = first - 3 + turn
        near = (key_block - block <= 1) & (block - key_block <= 1) & (block >= 2) & (block < block_total)
        allowed = ((turn < 2) | near) & (key_block >= 2)
        keys = block_rows(k_ref, first, 2)
        values = block_rows(v_ref, first, 2)
        dk_ref[here, :], dv_ref[here, :] = key_side(keys, values, blocks, allowed)

    pair_total = pair_ref[0]

    def random_pairs(step, carry):
        grads = []
        for k in range(4):
            number = 4 * step + k
            live = number < pair_total
            code = pair_ref[jnp.minimum(number, pair_total - 1) + 1]
            target = code // 65536
            block = code - target * 65536
            start = ((((target // 2) ^ place) >> 3) & 3) * rows + (target & 1) * BLOCK
            grads.append(
                (
                    pl.ds(pl.multiple_of(start, BLOCK), BLOCK),
                    key_side(block_rows(k_ref, target), block_rows(v_ref, target), (block,), live),
                )
            )
        for here, parts in grads:
            put(here, parts)
        return carry

    lax.fori_loop(0, (pair_total + 3) // 4, random_pairs, 0)

    @pl.when((place & ~24) == 0)
    def _():
        here = pl.ds(pl.multiple_of(group * rows, rows), rows)
        keys = block_rows(k_ref, 0, 2)
        values = block_rows(v_ref, 0, 2)

        def every(step, carry):
            put(here, key_side(keys, values, [4 * step + k for k in range(4)], None))
            return carry

        lax.fori_loop(0, block_total // 4, every, 0, unroll=4)

    data = lanes(rows) < SHARE
    for a in range(4):
        here = slice(rows * a, rows * (a + 1))
        grad_ref[here, :WIDE] = dq_ref[here, :]
        grad_ref[here, WIDE : 2 * WIDE] = jnp.where(data, dk_ref[here, :], 0.0).astype(bf16)
        grad_ref[here, 2 * WIDE :] = jnp.where(data, dv_ref[here, :], 0.0).astype(bf16)
    put_tokens(fast, tok_refs, tok_ref)
    tokens = tok_ref[...]
    grad = grad_ref[...]
    reduced = dense_right_t(tokens, down_ref[...]).astype(bf16)
    grad_reduced = dense_right_t(grad, up_ref[...]).astype(bf16)
    down_terms = dense_left_t(grad_reduced, tokens)
    up_terms = dense_left_t(reduced, grad)
    terms = [down_terms[RANK * j : RANK * (j + 1)] for j in range(3)]
    ups = []
    for j in range(3):
        up = up_terms[RANK * j : RANK * (j + 1), WIDE * j : WIDE * j + SHARE]
        ups.append(jnp.concatenate([jnp.where(group == g, up, 0.0) for g in range(4)], axis=1))
    terms += ups + [jnp.zeros((RANK, D), f32)] * 2
    core = (place >> 1) & 1
    quarter = plane_quarter(place)
    for part, value in enumerate(terms):
        early = early_ref[EARLY_PART * part : EARLY_PART * (part + 1), :]
        where = (((part // 4) ^ core) * 4 + ((part % 4) ^ quarter)) if fast else part
        terms_ref[where, :RANK] = value
        terms_ref[where, RANK:] = early
    near_ref[...] = terms_ref[:4]
    away_ref[...] = terms_ref[4:].astype(away_ref.dtype)
    for n, a in enumerate((0, 2, 1, 3)):
        here = slice(rows * a, rows * (a + 1))
        part = (dense_right_t(grad[here], w_ref[...]) + dense_mul(grad_reduced[here], down_ref[...])).astype(bf16)
        part_refs[n // 2][rows * (n % 2) : rows * (n % 2 + 1), :] = part


def normal(hidden):
    center = hidden - jnp.mean(hidden, axis=-1, keepdims=True)
    root = lax.rsqrt(jnp.mean(center * center, axis=-1, keepdims=True) + norm_eps)
    return center * root, root


def normal_back(grad, normed, root):
    mean = jnp.mean(grad, axis=-1, keepdims=True)
    return root * (grad - mean - normed * jnp.mean(grad * normed, axis=-1, keepdims=True))


def select_kernel(meta_ref, *refs):
    chosen = meta_ref[3]
    tables, (down_ref, up_ref, *rest) = refs[:6], refs[6:]
    down_ref[...] = tables[0][chosen, 3]
    up_ref[...] = tables[1][chosen, 3]
    for table, ref in zip(tables[2:], rest, strict=True):
        ref[...] = table[chosen]


def middle_kernel(
    fast,
    meta_ref,
    ctx_refs,
    tok_ref,
    cot_ref,
    late_hbm,
    gain_ref,
    down_ref,
    up_ref,
    inner_down_ref,
    inner_up_ref,
    outer_down_ref,
    outer_up_ref,
    wide_ref,
    out_ref,
    grad_ref,
    piece_refs,
    terms_ref,
    hold_ref,
    pre_ref,
    act_ref,
    late_ref,
    sems,
):
    group = meta_ref[2]
    rows = tok_ref.shape[0]
    share = D // (FF // D)
    places = [(slice(None), slice(D * c, D * (c + 1))) for c in range(1 + FF // D)]
    if fast:
        places += [(slice(share * c, share * (c + 1)), slice(D + FF, D + 2 * FF)) for c in range(FF // D)]
    copies = [
        pltpu.make_async_copy(late_hbm.at[place], late_ref.at[place], sems.at[n]) for n, place in enumerate(places)
    ]
    order = [0] + [n for c in range(FF // D) for n in (1 + c, 1 + FF // D + c) if n < len(copies)]
    for n in order:
        copies[n].start()

    def build(c):
        copies[1 + FF // D + c].wait()
        slab = 24
        for pair in range(share // (2 * slab)):
            first = share * c + 2 * slab * pair
            block = late_ref[first : first + 2 * slab, D + FF :].astype(f32)
            cut = [
                block[slab * side : slab * (side + 1), D * n : D * (n + 1)]
                for side in range(2)
                for n in range(FF // D)
            ]
            wide_ref[4 * first : 4 * first + 8 * slab, :] = jnp.concatenate(cut, axis=0).astype(bf16)

    for a in range(4):
        hold_ref[a] = ctx_refs[a][...]
    context = jnp.concatenate([hold_ref[group ^ g][:, :SHARE] for g in range(4)], axis=1)
    context_red = dense_right_t(context, down_ref[...]).astype(bf16)
    copies[0].wait()
    attended = dense_mul(context, late_ref[:, :D]) + dense_mul(context_red, up_ref[...])
    first, first_root = normal(tok_ref[...].astype(f32) + attended)
    first_norm = first * gain_ref[0:1, :] + gain_ref[1:2, :]
    first_low = first_norm.astype(bf16)
    inner_red = dense_right_t(first_low, inner_down_ref[...]).astype(bf16)
    outer_red = jnp.zeros((rows, RANK), f32)
    outer_out = jnp.zeros((rows, D), f32)
    for c in range(FF // D):
        here = slice(D * c, D * (c + 1))
        copies[1 + c].wait()
        if fast:
            build(c)
        pre = dense_mul(first_low, late_ref[:, D * (c + 1) : D * (c + 2)]) + dense_mul(
            inner_red, inner_up_ref[:, here]
        )
        pre_ref[:, here] = pre
        active = (0.5 * pre * (1.0 + lax.erf(pre * 0.7071067811865476))).astype(bf16)
        act_ref[:, here] = active
        outer_red = outer_red + dense_right_t(active, outer_down_ref[:, here])
        outer_out = outer_out + dense_mul(active, wide_ref[here, :])
    outer_red = outer_red.astype(bf16)
    outer_out = outer_out + dense_mul(outer_red, outer_up_ref[...])
    second, second_root = normal(first_norm + outer_out)
    position = meta_ref[0] * rows + lax.broadcasted_iota(jnp.int32, (rows, D), 0)
    valid = (position < meta_ref[1]).astype(f32)
    out_ref[...] = ((second * gain_ref[2:3, :] + gain_ref[3:4, :]) * valid).astype(bf16)
    grad_second = normal_back(valid * cot_ref[...].astype(f32) * gain_ref[2:3, :], second, second_root)
    grad_outer = grad_second.astype(bf16)
    first_up = RANK * 3
    first_down = RANK * (3 + FF // D)
    terms_ref[first_down + RANK * (FF // D) :, :] = dense_left_t(outer_red, grad_outer)
    outer_grad_red = dense_right_t(grad_outer, outer_up_ref[...]).astype(bf16)
    inner_grad_red = jnp.zeros((rows, RANK), f32)
    grad_first = grad_second
    for c in range(FF // D):
        here = slice(D * c, D * (c + 1))
        grad_active = dense_right_t(grad_outer, wide_ref[here, :]) + dense_mul(
            outer_grad_red, outer_down_ref[:, here]
        )
        pre = pre_ref[:, here]
        slope = 0.5 * (1.0 + lax.erf(pre * 0.7071067811865476)) + pre * (
            0.3989422804014327 * jnp.exp(-0.5 * pre * pre)
        )
        grad_inner = (slope * grad_active).astype(bf16)
        terms_ref[first_up + RANK * c : first_up + RANK * (c + 1), :] = dense_left_t(inner_red, grad_inner)
        terms_ref[first_down + RANK * c : first_down + RANK * (c + 1), :] = dense_left_t(
            outer_grad_red, act_ref[:, here]
        )
        inner_grad_red = inner_grad_red + dense_right_t(grad_inner, inner_up_ref[:, here])
        grad_first = grad_first + dense_right_t(grad_inner, late_ref[:, D * (c + 1) : D * (c + 2)])
    inner_grad_red = inner_grad_red.astype(bf16)
    terms_ref[2 * RANK : 3 * RANK, :] = dense_left_t(inner_grad_red, first_low)
    grad_first = grad_first + dense_mul(inner_grad_red, inner_down_ref[...])
    grad_attended = normal_back(grad_first * gain_ref[0:1, :], first, first_root)
    grad_ref[...] = grad_attended
    grad_low = grad_attended.astype(bf16)
    context_grad_red = dense_right_t(grad_low, up_ref[...]).astype(bf16)
    terms_ref[:RANK, :] = dense_left_t(context_grad_red, context)
    terms_ref[RANK : 2 * RANK, :] = dense_left_t(context_red, grad_low)
    grad_context = (
        dense_right_t(grad_low, late_ref[:, :D]) + dense_mul(context_grad_red, down_ref[...])
    ).astype(bf16)
    for g in range(4):
        hold_ref[group ^ g, :DENSE_ROWS, :] = fold_rows(grad_context[:, SHARE * g : SHARE * (g + 1)])
    for a in range(4):
        piece_refs[a][...] = hold_ref[a, :DENSE_ROWS, :]


def spread_kernel(meta_ref, *refs):
    part_refs = refs[:8]
    outs = refs[14:20]
    sum_ref, sems = refs[20:]
    quarter = plane_quarter(meta_ref[0])
    core = (meta_ref[0] >> 1) & 1
    chosen = meta_ref[3]
    for n in range(8):
        part = (core ^ (n // 4)) * 4 + (quarter ^ (n % 4))
        sum_ref[pl.ds(pl.multiple_of(part * RANK, RANK), RANK), :] = part_refs[n][:RANK, :].astype(f32)
        sum_ref[pl.ds(pl.multiple_of(LATE_ROWS + part * EARLY_PART, 8), EARLY_PART), :] = part_refs[n][RANK:, :].astype(f32)
    places = [outs[0].at[chosen, j] for j in range(3)] + [outs[1].at[chosen, j] for j in range(3)]
    places += [None, None, outs[0].at[chosen, 3], outs[1].at[chosen, 3], outs[2].at[chosen]]
    places += [outs[n].at[chosen, :, pl.ds(D * c, D)] for n in (3, 4) for c in range(FF // D)]
    places.append(outs[5].at[chosen])
    copies = [
        pltpu.make_async_copy(sum_ref.at[pl.ds(RANK * n, RANK), :], where, sems.at[n])
        for n, where in enumerate(places)
        if where is not None
    ]
    for copy in copies:
        copy.start()
    for copy in copies:
        copy.wait()


LATE_ROWS = 8 * RANK
EARLY_KINDS = 12
EARLY_PART = EARLY_KINDS * RANK // 8
ANY = pl.BlockSpec(memory_space=pl.ANY)
SMEM = pl.BlockSpec(memory_space=pltpu.SMEM)
VMEM = pl.BlockSpec(memory_space=pltpu.VMEM)


def shards(
    tokens,
    cotangent,
    w_query,
    w_key,
    w_value,
    w_output,
    w_inner,
    w_outer,
    gain_first,
    shift_first,
    gain_second,
    shift_second,
    attn_down,
    attn_up,
    inner_down,
    inner_up,
    outer_down,
    outer_up,
    lengths,
    rand_blocks,
    adapter_pick,
):
    device_total = lax.axis_size("seq") * lax.axis_size("head")
    local_rows = tokens.shape[0]
    seq_total = lengths.shape[0]
    members = device_total // seq_total
    rows_total = members * local_rows
    block_total = rows_total // BLOCK
    chunk = 4 * local_rows
    index = lax.axis_index("seq") * lax.axis_size("head") + lax.axis_index("head")
    place = index % members
    seq_number = index // members
    group = (place >> 3) & 3
    seq_length = lengths[seq_number]
    chosen = adapter_pick[seq_number]
    fast = device_total == 32 and members == 32
    together = lax.optimization_barrier

    def send(value, even, odd):
        return lax.ppermute(
            value, AXES, [(j, j ^ (odd if (j >> 1) & 1 else even)) for j in range(device_total)]
        )

    def swap(value, mask):
        return send(value, mask, mask)

    def one(value):
        return send(value, 4, 1)

    def two(value):
        return send(value, 1, 4)

    def exchange(pieces, masks=PEERS):
        return [pieces[0]] + [swap(pieces[a], masks[a]) for a in range(1, 4)]

    def gather_start(value):
        if not fast:
            masks = [slab_offset(n, place, False) for n in range(members // 4)]
            return [value] + [swap(value, mask) for mask in masks[1:]]
        return [value, one(value), two(value)]

    def gather_end(slabs):
        if not fast:
            return slabs
        slabs = slabs + [two(slabs[1])]
        return slabs + [swap(slab, 2) for slab in slabs]

    def gather_direct(value):
        return gather_start(value) + ([swap(value, 5)] if fast else [])

    def gather_hand(slabs):
        return slabs + [swap(slab, 2) for slab in slabs] if fast else slabs

    def gather_all(value):
        return lax.all_gather(value, AXES, axis=0, tiled=True)

    def share_columns(table, which=group):
        return lax.dynamic_slice_in_dim(table, which * SHARE, SHARE, table.ndim - 1)

    slab = D // device_total
    meta = jnp.stack([place, seq_length, group, chosen]).astype(jnp.int32)
    if fast:
        late_local, *slices = pl.pallas_call(
            pack_kernel,
            in_specs=[SMEM] + [VMEM] * 6,
            out_specs=[VMEM] * 5,
            out_shape=[jax.ShapeDtypeStruct((slab, D + 2 * FF), bf16)]
            + [jax.ShapeDtypeStruct((slab, 3 * WIDE), bf16)] * 4,
            name="pack",
        )(rand_blocks, w_query, w_key, w_value, w_output, w_inner, w_outer)
        late = gather_all(late_local)
        mine = exchange(slices)
        far_tokens = swap(tokens, PEERS[2])
        near_tokens = swap(jnp.concatenate([tokens, far_tokens], axis=0), PEERS[1])
        token_refs = [tokens, far_tokens, near_tokens]
        w_slabs = gather_hand(gather_direct(jnp.concatenate(mine, axis=0)))
    else:
        late = gather_all(
            jnp.concatenate([w_output, w_inner] + [w_outer[slab * c : slab * (c + 1)] for c in range(FF // D)], axis=1)
        )
        full_qkv = gather_all(jnp.concatenate([w_query, w_key, w_value], axis=1))
        rand_all = lax.all_gather(rand_blocks, "seq", axis=0, tiled=True)
        rand_flat = lax.dynamic_slice_in_dim(rand_all, seq_number * block_total, block_total, 0).reshape(-1)
        token_refs = exchange([tokens] * 4)
        w_slabs = [
            jnp.concatenate(
                [
                    jnp.pad(share_columns(full_qkv[:, D * j : D * (j + 1)]), ((0, 0), (0, WIDE - SHARE)))
                    for j in range(3)
                ],
                axis=1,
            )
        ]

    wide_rows = jax.ShapeDtypeStruct((rows_total, WIDE), bf16)
    piece_shapes = [jax.ShapeDtypeStruct((local_rows, WIDE), bf16)] * 4
    side_weight, down_stack, up_stack, query_own, pair_own, rand_table = pl.pallas_call(
        functools.partial(project_kernel, fast),
        in_specs=[SMEM] + [VMEM] * (2 + len(token_refs) + len(w_slabs)),
        out_specs=[VMEM] * 6,
        out_shape=[
            jax.ShapeDtypeStruct((D, 3 * WIDE), bf16),
            jax.ShapeDtypeStruct((WIDE // 2, D), bf16),
            jax.ShapeDtypeStruct((WIDE // 2, 3 * WIDE), bf16),
            jax.ShapeDtypeStruct((chunk, WIDE), bf16),
            jax.ShapeDtypeStruct((chunk, 2 * SHARE), bf16),
            jax.ShapeDtypeStruct((32, WIDE // 2), jnp.int32),
        ],
        scratch_shapes=[
            pltpu.VMEM((3, WIDE // 2, WIDE), bf16),
            pltpu.VMEM((chunk, D), bf16),
            pltpu.VMEM((D, 3 * WIDE), f32),
        ],
        compiler_params=pltpu.CompilerParams(vmem_limit_bytes=VMEM_LIMIT),
        name="project",
    )(meta, attn_down, attn_up, *token_refs, *w_slabs)
    if fast:
        rand_flat = rand_table
    pair_list = pl.pallas_call(
        functools.partial(collect_kernel, fast, block_total),
        in_specs=[SMEM, SMEM],
        out_specs=SMEM,
        out_shape=jax.ShapeDtypeStruct((3 * block_total + 8,), jnp.int32),
        name="collect",
    )(meta, rand_flat)
    pair_slabs = gather_start(pair_own)
    pair_list, pair_slabs[1] = together((pair_list, pair_slabs[1]))
    pair_slabs = gather_end(pair_slabs)
    key_all, value_all, *ctx, aux = pl.pallas_call(
        functools.partial(attend_kernel, fast),
        in_specs=[SMEM, SMEM] + [VMEM] * (1 + len(pair_slabs)),
        out_specs=[VMEM] * 7,
        out_shape=[wide_rows] * 2 + piece_shapes + [jax.ShapeDtypeStruct((chunk, WIDE), f32)],
        scratch_shapes=[pltpu.VMEM((rows_total // chunk, (2 if fast else 1) * STACK, chunk), f32)],
        compiler_params=pltpu.CompilerParams(vmem_limit_bytes=VMEM_LIMIT),
        name="attend",
    )(meta, rand_flat, query_own, *pair_slabs)
    *tables, ctx[1] = together((attn_down, attn_up, inner_down, inner_up, outer_down, outer_up, ctx[1]))
    ctx_pieces = exchange(ctx)

    gains = jnp.stack([gain_first, shift_first, gain_second, shift_second])
    chosen_maps = pl.pallas_call(
        select_kernel,
        in_specs=[SMEM] + [VMEM] * 6,
        out_specs=[VMEM] * 6,
        out_shape=[jax.ShapeDtypeStruct((RANK, width), bf16) for width in (D, D, D, FF, FF, D)],
        name="select",
    )(meta, *tables)
    *chosen_maps, late = together((*chosen_maps, late))
    middle_in = [tokens, cotangent, late, gains, *chosen_maps]
    wide_shape = [pltpu.VMEM((FF, D), bf16)]
    if not fast:
        middle_in.append(
            late[:, D + FF :].reshape(device_total, slab, FF // D, D).transpose(0, 2, 1, 3).reshape(FF, D)
        )
        wide_shape = []
    count = len(middle_in)

    def middle(meta_ref, *refs):
        ins, outs, scratch = refs[4 : 4 + count], refs[4 + count : 11 + count], refs[11 + count :]
        wide_ref = scratch[-1] if fast else ins[-1]
        middle_kernel(
            fast, meta_ref, refs[:4], *ins[:10], wide_ref, *outs[:2], outs[2:6], outs[6], *scratch[:5]
        )


    output, grad_attended, *grad_pieces, early_terms = pl.pallas_call(
        middle,
        in_specs=[SMEM] + [VMEM] * 6 + [ANY] + [VMEM] * (count - 3),
        out_specs=[VMEM] * 7,
        out_shape=[
            jax.ShapeDtypeStruct((local_rows, D), bf16),
            jax.ShapeDtypeStruct((local_rows, D), f32),
        ]
        + [jax.ShapeDtypeStruct((DENSE_ROWS, WIDE), bf16)] * 4
        + [jax.ShapeDtypeStruct((EARLY_KINDS * RANK, D), f32)],
        scratch_shapes=[
            pltpu.VMEM((4, local_rows, WIDE), bf16),
            pltpu.VMEM((local_rows, FF), f32),
            pltpu.VMEM((local_rows, FF), bf16),
            pltpu.VMEM(late.shape, bf16),
            pltpu.SemaphoreType.DMA((1 + 2 * (FF // D),)),
        ]
        + wide_shape,
        compiler_params=pltpu.CompilerParams(vmem_limit_bytes=VMEM_LIMIT),
        name="middle",
    )(meta, *ctx_pieces, *middle_in)
    query_send, grad_pieces[0] = together((query_own, grad_pieces[0]))
    query_slabs = gather_hand(gather_direct(query_send))
    grad_wide = pl.pallas_call(
        delta_kernel,
        in_specs=[VMEM] * 5,
        out_specs=VMEM,
        out_shape=jax.ShapeDtypeStruct((chunk, WIDE), bf16),
        name="delta",
    )(*exchange(grad_pieces), aux)
    def reduced(terms):
        paired = terms[0] + swap(terms[1], 2)
        moved = exchange([paired[a] for a in range(4)])
        part = (moved[0] + moved[1]) + (moved[2] + moved[3])
        moved = [part] + [swap(part, depth) for depth in DEPTHS[1:]]
        return (moved[0] + moved[1]) + (moved[2] + moved[3])

    grad_slabs = gather_start(grad_wide)
    out_shapes = [
        jax.ShapeDtypeStruct(shape, f32)
        for shape in (
            (ADAPTERS, 4, RANK, D),
            (ADAPTERS, 4, RANK, D),
            (ADAPTERS, RANK, D),
            (ADAPTERS, RANK, FF),
            (ADAPTERS, RANK, FF),
            (ADAPTERS, RANK, D),
        )
    ]
    zero_shapes = out_shapes if fast else []
    query_grad, *zeros = pl.pallas_call(
        functools.partial(near_kernel, fast),
        in_specs=[SMEM, SMEM] + [VMEM] * 4,
        out_specs=[VMEM] + [ANY] * len(zero_shapes),
        out_shape=[jax.ShapeDtypeStruct((chunk, WIDE), bf16)] + zero_shapes,
        scratch_shapes=[pltpu.VMEM((4, RANK, D), f32), pltpu.SemaphoreType.DMA((ADAPTERS * 12,))],
        compiler_params=pltpu.CompilerParams(vmem_limit_bytes=VMEM_LIMIT),
        cost_estimate=pl.CostEstimate(flops=12000000000, bytes_accessed=8000000, transcendentals=1000000),
        name="near",
    )(meta, rand_flat, query_own, key_all, value_all, grad_wide)
    query_grad, *grad_slabs = together((query_grad, *grad_slabs))
    grad_slabs = gather_end(grad_slabs)
    kept, given, near_terms, away_terms = pl.pallas_call(
        functools.partial(far_kernel, fast),
        in_specs=[SMEM, SMEM] + [VMEM] * (7 + len(token_refs) + 2 * len(grad_slabs)),
        out_specs=[VMEM] * 4,
        out_shape=[jax.ShapeDtypeStruct((2 * local_rows, D), bf16)] * 2
        + [jax.ShapeDtypeStruct((4, RANK + EARLY_PART, D), kind) for kind in (f32, bf16 if fast else f32)],
        scratch_shapes=[
            pltpu.VMEM((rows_total, WIDE), bf16),
            pltpu.VMEM((rows_total, WIDE), bf16),
            pltpu.VMEM((chunk, WIDE), f32),
            pltpu.VMEM((chunk, WIDE), f32),
            pltpu.VMEM((chunk, 3 * WIDE), bf16),
            pltpu.VMEM((chunk, D), bf16),
            pltpu.VMEM((8, RANK + EARLY_PART, D), f32),
        ],
        compiler_params=pltpu.CompilerParams(vmem_limit_bytes=VMEM_LIMIT),
        name="far",
    )(
        meta,
        pair_list,
        key_all,
        value_all,
        query_grad,
        side_weight,
        down_stack,
        up_stack,
        early_terms,
        *token_refs,
        *query_slabs,
        *grad_slabs,
    )
    kept = kept.astype(f32) + swap(given, PEERS[1]).astype(f32)
    passed = swap(kept[local_rows:].astype(bf16), PEERS[2])
    grad_tokens = grad_attended + (kept[:local_rows] + passed.astype(f32))

    if fast:
        paired = near_terms + swap(away_terms, 2).astype(f32)
        moved = [paired[0]] + [swap(paired[a].astype(bf16), PLANE[a]).astype(f32) for a in range(1, 4)]
        part = ((moved[0] + moved[1]) + (moved[2] + moved[3])).astype(bf16)
        moved = [piece.astype(f32) for piece in exchange([part] * 4)]
        part = ((moved[0] + moved[1]) + (moved[2] + moved[3])).astype(bf16)
        part_list = exchange([part] * 4, PLANE)
        part_list = part_list + [swap(value, 2) for value in part_list]
        sums = pl.pallas_call(
            spread_kernel,
            in_specs=[SMEM] + [VMEM] * 8 + [ANY] * 6,
            out_specs=[ANY] * 6,
            out_shape=out_shapes,
            scratch_shapes=[
                pltpu.VMEM((LATE_ROWS + EARLY_KINDS * RANK, D), f32),
                pltpu.SemaphoreType.DMA((8 + EARLY_KINDS,)),
            ],
            input_output_aliases={9 + n: n for n in range(6)},
            name="spread",
        )(meta, *part_list, *zeros)
        return (output, grad_tokens, *sums)

    terms = jnp.concatenate([near_terms, away_terms], axis=0)
    terms = jnp.concatenate([terms[:, :RANK].reshape(-1, D), terms[:, RANK:].reshape(-1, D)], axis=0)
    slots = (jnp.arange(seq_total) == seq_number).astype(f32)[:, None, None]
    every = lax.psum(slots * terms[None], AXES)

    def spread(kinds, width):
        def term(s):
            rows = jnp.concatenate([every[s, kind * RANK : (kind + width // D) * RANK] for kind in kinds], axis=0)
            value = rows.reshape(len(kinds), width // D, RANK, D).transpose(0, 2, 1, 3)
            value = value.reshape(len(kinds), RANK, width)
            return (jnp.arange(ADAPTERS) == adapter_pick[s]).astype(f32)[:, None, None, None] * value[None]

        return functools.reduce(lambda x, y: x + y, [term(s) for s in range(seq_total)])

    wide = FF // D
    sums = [
        spread((0, 1, 2, 8), D),
        spread((3, 4, 5, 9), D),
        spread((10,), D),
        spread((11,), FF),
        spread((11 + wide,), FF),
        spread((11 + 2 * wide,), D),
    ]
    return (
        output,
        grad_tokens,
        *[value.reshape(leaf.shape) for value, leaf in zip(sums, out_shapes, strict=True)],
    )


def solution(mesh):
    rows = P(AXES, None)
    placed = (rows,) * 8 + (P(),) * 11 + (P("seq", None), P())
    return jax.shard_map(
        shards,
        mesh=mesh,
        in_specs=placed,
        out_specs=(rows, rows) + (P(),) * 6,
        check_vma=False,
    )
```

profile of v0, /device:TPU:0, one launch (start us, length us, event | category | flops | bytes accessed | tf_op | source)
XLA Modules:
  0.0 219.6 jit_solution(1470200229796484270)
XLA Ops:
  7.2 2.8 %pack.1 = (bf16[24,6912]{1,0:T(8,128)(2,1)}, bf16[24,768]{1,0:T(8,128)(2,1)}, bf16[24,768]{1,0:T(8,128)(2,1)}, bf16[24,768]{1,0:T(8,128)(2,1)}, bf16[24,768]{1,0:T(8,128)(2,1)}) custom-call(s32[4,3]{1,0:T(4,128)} %rand_ref.1, bf16[24,768]{1,0:T(8,128)(2,1)} %query_ref.1, bf16[24,768]{1,0:T(8,128)(2,1)} %key_ref.1, bf16[24,768]{1,0:T(8,128)(2,1)} %value_ref.1, ...), custom_call_target="tpu_custom_call" | custom-call | tf_op jit(solution)/shard_map/pack/pallas_call | solution.py:854
  10.0 4.1 %collective-permute-start = (bf16[128,768]{1,0:T(8,128)(2,1)}, bf16[128,768]{1,0:T(8,128)(2,1)S(1)}, u32[]{:S(2)}, u32[]{:S(2)}) collective-permute-start(bf16[128,768]{1,0:T(8,128)(2,1)} %refs_0_.4), channel_id=1, source_target_pairs={{0,16},{1,17},{2,18},{3,19},{4,20},{5,21},{6,22},{7,23},{8,24},{9,... | collective-permute-start | bytes 589832 | tf_op jit(solution)/shard_map/ppermute | solution.py:811
  14.1 1.6 collective-permute-start.2
  16.0 2.5 %collective-permute-start.4 = (bf16[24,768]{1,0:T(8,128)(2,1)}, bf16[24,768]{1,0:T(8,128)(2,1)S(1)}, u32[]{:S(2)}, u32[]{:S(2)}) collective-permute-start(bf16[24,768]{1,0:T(8,128)(2,1)} %get-tuple-element.81), channel_id=1, source_target_pairs={{0,24},{1,25},{2,26},{3,27},{4,28},{5,29},{6,30},{7,31},{8,16},{9,... | collective-permute-start | bytes 110600 | tf_op jit(solution)/shard_map/ppermute | solution.py:811
  20.2 6.1 %collective-permute-done.3 = bf16[24,768]{1,0:T(8,128)(2,1)S(1)} collective-permute-done((bf16[24,768]{1,0:T(8,128)(2,1)}, bf16[24,768]{1,0:T(8,128)(2,1)S(1)}, u32[]{:S(2)}, u32[]{:S(2)}) %collective-permute-start.3) | collective-permute-done | bytes 36896 | tf_op jit(solution)/shard_map/ppermute | solution.py:811
  26.4 1.0 pad_maximum_fusion
  27.4 3.2 %collective-permute-start.1 = (bf16[256,768]{1,0:T(8,128)(2,1)S(1)}, bf16[256,768]{1,0:T(8,128)(2,1)S(1)}, u32[]{:S(2)}, u32[]{:S(2)}) collective-permute-start(bf16[256,768]{1,0:T(8,128)(2,1)S(1)} %pad_maximum_fusion), channel_id=1, source_target_pairs={{0,8},{1,9},{2,10},{3,11},{4,12},{5,13},{6,14},{7,15},{8,0},{9,1},... | collective-permute-start | bytes 1179656 | tf_op jit(solution)/shard_map/ppermute | solution.py:811
  30.7 1.5 collective-permute-start.5
  32.2 1.5 collective-permute-start.6
  34.2 3.2 %collective-permute-done.5.refs_4_ = bf16[96,768]{1,0:T(8,128)(2,1)S(1)} collective-permute-done((bf16[96,768]{1,0:T(8,128)(2,1)S(1)}, bf16[96,768]{1,0:T(8,128)(2,1)S(1)}, u32[]{:S(2)}, u32[]{:S(2)}) %collective-permute-start.5) | collective-permute-done | bytes 147488 | tf_op jit(solution)/shard_map/ppermute | solution.py:811
  37.5 3.0 %collective-permute-done.6.refs_5_ = bf16[96,768]{1,0:T(8,128)(2,1)S(1)} collective-permute-done((bf16[96,768]{1,0:T(8,128)(2,1)S(1)}, bf16[96,768]{1,0:T(8,128)(2,1)S(1)}, u32[]{:S(2)}, u32[]{:S(2)}) %collective-permute-start.6) | collective-permute-done | bytes 147488 | tf_op jit(solution)/shard_map/ppermute | solution.py:811
  44.5 4.7 %project.1 = (bf16[768,768]{1,0:T(8,128)(2,1)}, bf16[128,768]{1,0:T(8,128)(2,1)}, bf16[128,768]{1,0:T(8,128)(2,1)}, bf16[512,256]{1,0:T(8,128)(2,1)}, bf16[512,384]{1,0:T(8,128)(2,1)}, /*index=5*/s32[32,128]{1,0:T(8,128)}) custom-call(s32[4]{0:T(128)} %pad_add_fusion.meta_ref, bf16[8,4,16,768]{3,2,1,0:T(8,128)(2,1)} %refs_0_.3, ...), custom_call_target="tpu_custom_call" | custom-call | tf_op jit(solution)/shard_map/project/pallas_call | solution.py:888
  50.1 1.5 collective-permute-start.13
  51.6 3.8 %collect.1.pair_ref = s32[200]{0:T(256)} custom-call(s32[4]{0:T(128)} %pad_add_fusion.meta_ref, s32[32,128]{1,0:T(8,128)} %get-tuple-element.82.rand_ref), custom_call_target="tpu_custom_call" | custom-call | tf_op jit(solution)/shard_map/collect/pallas_call | solution.py:910
  55.4 7.0 %collective-permute-done.12.refs_1_ = bf16[512,384]{1,0:T(8,128)(2,1)S(1)} collective-permute-done((bf16[512,384]{1,0:T(8,128)(2,1)}, bf16[512,384]{1,0:T(8,128)(2,1)S(1)}, u32[]{:S(2)}, u32[]{:S(2)}) %collective-permute-start.12) | collective-permute-done | bytes 393248 | tf_op jit(solution)/shard_map/ppermute | solution.py:811
  62.4 1.8 collective-permute-start.14
  64.8 7.3 %collective-permute-done.14.refs_3_ = bf16[512,384]{1,0:T(8,128)(2,1)S(1)} collective-permute-done((bf16[512,384]{1,0:T(8,128)(2,1)S(1)}, bf16[512,384]{1,0:T(8,128)(2,1)S(1)}, u32[]{:S(2)}, u32[]{:S(2)}) %collective-permute-start.14) | collective-permute-done | bytes 393248 | tf_op jit(solution)/shard_map/ppermute | solution.py:811
  72.2 1.6 collective-permute-done.18.refs_7_
  74.6 14.9 %attend.1 = (bf16[4096,256]{1,0:T(8,128)(2,1)}, bf16[4096,256]{1,0:T(8,128)(2,1)}, bf16[128,256]{1,0:T(8,128)(2,1)}, bf16[128,256]{1,0:T(8,128)(2,1)}, bf16[128,...) custom-call(s32[4]{0:T(128)} %pad_add_fusion.meta_ref, s32[32,128]{1,0:T(8,128)} %get-tuple-element.82.rand_ref, ...), custom_call_target="tpu_custom_call" | custom-call | tf_op jit(solution)/shard_map/attend/pallas_call | solution.py:920
  89.5 1.1 collective-permute-start.19
  90.5 1.6 collective-permute-start.20
  92.2 1.7 collective-permute-start.21
  94.5 2.7 %select.7 = (bf16[16,768]{1,0:T(8,128)(2,1)}, bf16[16,768]{1,0:T(8,128)(2,1)}, bf16[16,768]{1,0:T(8,128)(2,1)}, bf16[16,3072]{1,0:T(8,128)(2,1)}, bf16[16,3072]{1,0:T(8,128)(2,1)}, /*index=5*/bf16[16,768]{1,0:T(8,128)(2,1)}) custom-call(s32[4]{0:T(128)} %pad_add_fusion.meta_ref, bf16[8,4,16,768]{3,2,1,0:T(8,128)(2,1)} %refs_0_.3, ...), custom_call_target="tpu_custom_call" | custom-call | tf_op jit(solution)/shard_map/select/pallas_call | solution.py:933
  97.2 10.8 %all-gather.2.cloned.1.call-done.refs_6_ = bf16[768,6912]{1,0:T(8,128)(2,1)} async-done(((bf16[24,6912]{1,0:T(8,128)(2,1)}), bf16[768,6912]{1,0:T(8,128)(2,1)}) %all-gather.2.cloned.1.call-update) | async-done | bytes 10616848 | tf_op jit(solution)/shard_map/all_gather | solution.py:846
  108.6 13.7 %middle.1 = (bf16[128,768]{1,0:T(8,128)(2,1)}, f32[128,768]{1,0:T(8,128)}, bf16[96,256]{1,0:T(8,128)(2,1)}, bf16[96,256]{1,0:T(8,128)(2,1)}, bf16[96,256]{1,0:T(...) custom-call(s32[4]{0:T(128)} %pad_add_fusion.meta_ref, bf16[128,256]{1,0:T(8,128)(2,1)} %get-tuple-element.86.refs_0_, ...), custom_call_target="tpu_custom_call" | custom-call | tf_op jit(solution)/shard_map/middle/pallas_call | solution.py:958
  122.3 1.9 collective-permute-start.23
  124.3 2.4 %collective-permute-start.24 = (bf16[96,256]{1,0:T(8,128)(2,1)}, bf16[96,256]{1,0:T(8,128)(2,1)S(1)}, u32[]{:S(2)}, u32[]{:S(2)}) collective-permute-start(bf16[96,256]{1,0:T(8,128)(2,1)} %get-tuple-element.120), channel_id=1, source_target_pairs={{0,24},{1,25},{2,26},{3,27},{4,28},{5,29},{6,30},{7,31},{8,16},{9,... | collective-permute-start | bytes 147464 | tf_op jit(solution)/shard_map/ppermute | solution.py:811
  126.7 1.0 collective-permute-start.27
  127.8 1.5 collective-permute-start.28
  131.0 2.8 %delta.1.g_ref.refs_11_ = bf16[512,256]{1,0:T(8,128)(2,1)} custom-call(bf16[96,256]{1,0:T(8,128)(2,1)} %get-tuple-element.117.refs_0_, bf16[96,256]{1,0:T(8,128)(2,1)} %copy-done.47, bf16[96,256]{1,0:T(8,128)(2,1)} %copy-done.48, bf16[96,256]{1,0:T(8,128)(2,1)} %copy-done.49, f32[512,256]{1,0:T(8,128)} %get-tuple-element.121.refs_4_), custom_call_target="tpu_custom_call" | custom-call | tf_op jit(solution)/shard_map/delta/pallas_call | solution.py:981
  133.8 1.4 collective-permute-start.25
  135.2 1.3 collective-permute-start.26
  136.4 10.5 %near.1 = (bf16[512,256]{1,0:T(8,128)(2,1)}, f32[8,4,16,768]{3,2,1,0:T(8,128)}, f32[8,4,16,768]{3,2,1,0:T(8,128)}, f32[8,16,768]{2,1,0:T(8,128)}, f32[8,16,3072]...) custom-call(s32[4]{0:T(128)} %pad_add_fusion.meta_ref, s32[32,128]{1,0:T(8,128)} %get-tuple-element.82.rand_ref, ...), custom_call_target="tpu_custom_call" | custom-call | flops 12000000000 | bytes 8000000 | tf_op jit(solution)/shard_map/near/pallas_call | solution.py:1008
  147.6 1.0 collective-permute-start.34
  149.7 4.3 %collective-permute-done.34.refs_14_ = bf16[512,256]{1,0:T(8,128)(2,1)S(1)} collective-permute-done((bf16[512,256]{1,0:T(8,128)(2,1)S(1)}, bf16[512,256]{1,0:T(8,128)(2,1)S(1)}, u32[]{:S(2)}, u32[]{:S(2)}) %collective-permute-start.34) | collective-permute-done | bytes 262176 | tf_op jit(solution)/shard_map/ppermute | solution.py:811
  154.1 1.5 collective-permute-done.38.refs_18_
  156.3 22.6 %far.1 = (bf16[256,768]{1,0:T(8,128)(2,1)}, bf16[256,768]{1,0:T(8,128)(2,1)}, f32[4,40,768]{2,1,0:T(8,128)}, bf16[4,40,768]{2,1,0:T(8,128)(2,1)}) custom-call(s32[4]{0:T(128)} %pad_add_fusion.meta_ref, s32[200]{0:T(256)} %collect.1.pair_ref, bf16[4096,256]{1,0:T(8,128)(2,1)} %get-tuple-element.114.k_ref, bf16[4096,256]{1,0:T(8,128)(2,1)} %get-tuple-element.115.v_ref, ...), custom_call_target="tpu_custom_call" | custom-call | tf_op jit(solution)/shard_map/far/pallas_call | solution.py:1020
  179.6 1.0 collective-permute-done.41
  180.7 1.1 fusion.4
  181.9 3.4 %collective-permute-start.42 = (bf16[40,768]{1,0:T(8,128)(2,1)S(1)}, bf16[40,768]{1,0:T(8,128)(2,1)S(1)}, u32[]{:S(2)}, u32[]{:S(2)}) collective-permute-start(bf16[40,768]{1,0:T(8,128)(2,1)S(1)} %get-tuple-element.150), channel_id=1, source_target_pairs={{0,1},{1,0},{2,3},{3,2},{4,5},{5,4},{6,7},{7,6},{8,9},{9,8},{10,11... | collective-permute-start | bytes 184328 | tf_op jit(solution)/shard_map/ppermute | solution.py:811
  185.3 2.1 collective-permute-done.44
  188.1 2.4 %collective-permute-start.47 = (bf16[40,768]{1,0:T(8,128)(2,1)S(1)}, bf16[40,768]{1,0:T(8,128)(2,1)S(1)}, u32[]{:S(2)}, u32[]{:S(2)}) collective-permute-start(bf16[40,768]{1,0:T(8,128)(2,1)S(1)} %fusion.3), channel_id=1, source_target_pairs={{0,24},{1,25},{2,26},{3,27},{4,28},{5,29},{6,30},{7,31},{8,16},{9,... | collective-permute-start | bytes 184328 | tf_op jit(solution)/shard_map/ppermute | solution.py:811
  190.5 2.1 collective-permute-start.45
  194.3 6.4 %collective-permute-done.46 = bf16[40,768]{1,0:T(8,128)(2,1)S(1)} collective-permute-done((bf16[40,768]{1,0:T(8,128)(2,1)S(1)}, bf16[40,768]{1,0:T(8,128)(2,1)S(1)}, u32[]{:S(2)}, u32[]{:S(2)}) %collective-permute-start.46) | collective-permute-done | bytes 61472 | tf_op jit(solution)/shard_map/ppermute | solution.py:811
  200.8 1.9 collective-permute-start.48
  202.7 1.6 collective-permute-start.50
  205.1 1.9 collective-permute-done.49.refs_2_
  209.7 2.2 %spread.1 = (f32[8,4,16,768]{3,2,1,0:T(8,128)}, f32[8,4,16,768]{3,2,1,0:T(8,128)}, f32[8,16,768]{2,1,0:T(8,128)}, f32[8,16,3072]{2,1,0:T(8,128)}, f32[8,16,3072]{2,1,0:T(8,128)}, /*index=5*/f32[8,16,768]{2,1,0:T(8,128)}) custom-call(s32[4]{0:T(128)} %pad_add_fusion.meta_ref, ...), custom_call_target="tpu_custom_call", output_to_operand_aliasing={{0}: (9, {}), {1}: (10, {}), {2}: (11, {}), {3}: (12, {}), ... | custom-call | tf_op jit(solution)/shard_map/spread/pallas_call | solution.py:1063
  (201 shorter events, 20.6 us)
Async XLA Ops:
  7.2 100.7 %all-gather.2.cloned.1.call-start = ((), (), s32[]{:S(2)}) async-start(), calls=%async_computation | async-start | bytes 10948608 | tf_op jit(solution)/shard_map/all_gather | solution.py:846
  10.0 16.3 %collective-permute-start = (bf16[128,768]{1,0:T(8,128)(2,1)}, bf16[128,768]{1,0:T(8,128)(2,1)S(1)}, u32[]{:S(2)}, u32[]{:S(2)}) collective-permute-start(bf16[128,768]{1,0:T(8,128)(2,1)} %refs_0_.4), channel_id=1, source_target_pairs={{0,16},{1,17},{2,18},{3,19},{4,20},{5,21},{6,22},{7,23},{8,24},{9,... | collective-permute-start | bytes 589832 | tf_op jit(solution)/shard_map/ppermute | solution.py:811
  14.1 6.1 %collective-permute-start.2 = (bf16[24,768]{1,0:T(8,128)(2,1)}, bf16[24,768]{1,0:T(8,128)(2,1)S(1)}, u32[]{:S(2)}, u32[]{:S(2)}) collective-permute-start(bf16[24,768]{1,0:T(8,128)(2,1)} %get-tuple-element.79), channel_id=1, source_target_pairs={{0,8},{1,9},{2,10},{3,11},{4,12},{5,13},{6,14},{7,15},{8,0},{9,1},... | collective-permute-start | bytes 110600 | tf_op jit(solution)/shard_map/ppermute | solution.py:811
  15.7 10.7 %collective-permute-start.3 = (bf16[24,768]{1,0:T(8,128)(2,1)}, bf16[24,768]{1,0:T(8,128)(2,1)S(1)}, u32[]{:S(2)}, u32[]{:S(2)}) collective-permute-start(bf16[24,768]{1,0:T(8,128)(2,1)} %get-tuple-element.80), channel_id=1, source_target_pairs={{0,16},{1,17},{2,18},{3,19},{4,20},{5,21},{6,22},{7,23},{8,24},{9,... | collective-permute-start | bytes 110600 | tf_op jit(solution)/shard_map/ppermute | solution.py:811
  16.0 14.6 %collective-permute-start.4 = (bf16[24,768]{1,0:T(8,128)(2,1)}, bf16[24,768]{1,0:T(8,128)(2,1)S(1)}, u32[]{:S(2)}, u32[]{:S(2)}) collective-permute-start(bf16[24,768]{1,0:T(8,128)(2,1)} %get-tuple-element.81), channel_id=1, source_target_pairs={{0,24},{1,25},{2,26},{3,27},{4,28},{5,29},{6,30},{7,31},{8,16},{9,... | collective-permute-start | bytes 110600 | tf_op jit(solution)/shard_map/ppermute | solution.py:811
  27.4 15.6 %collective-permute-start.1 = (bf16[256,768]{1,0:T(8,128)(2,1)S(1)}, bf16[256,768]{1,0:T(8,128)(2,1)S(1)}, u32[]{:S(2)}, u32[]{:S(2)}) collective-permute-start(bf16[256,768]{1,0:T(8,128)(2,1)S(1)} %pad_maximum_fusion), channel_id=1, source_target_pairs={{0,8},{1,9},{2,10},{3,11},{4,12},{5,13},{6,14},{7,15},{8,0},{9,1},... | collective-permute-start | bytes 1179656 | tf_op jit(solution)/shard_map/ppermute | solution.py:811
  30.7 6.8 %collective-permute-start.5 = (bf16[96,768]{1,0:T(8,128)(2,1)S(1)}, bf16[96,768]{1,0:T(8,128)(2,1)S(1)}, u32[]{:S(2)}, u32[]{:S(2)}) collective-permute-start(bf16[96,768]{1,0:T(8,128)(2,1)S(1)} %constant_dynamic-update-slice_fusion.refs_3_), channel_id=1, source_target_pairs={{0,4},{1,5},{2,3},{3,2},{4,0},{5,1},{6,7},{7,6},{8,12},{9,13},{10,... | collective-permute-start | bytes 442376 | tf_op jit(solution)/shard_map/ppermute | solution.py:811
  32.2 8.3 %collective-permute-start.6 = (bf16[96,768]{1,0:T(8,128)(2,1)S(1)}, bf16[96,768]{1,0:T(8,128)(2,1)S(1)}, u32[]{:S(2)}, u32[]{:S(2)}) collective-permute-start(bf16[96,768]{1,0:T(8,128)(2,1)S(1)} %constant_dynamic-update-slice_fusion.refs_3_), channel_id=1, source_target_pairs={{0,1},{1,0},{2,6},{3,7},{4,5},{5,4},{6,2},{7,3},{8,9},{9,8},{10,14... | collective-permute-start | bytes 442376 | tf_op jit(solution)/shard_map/ppermute | solution.py:811
  33.7 6.8 %collective-permute-start.7 = (bf16[96,768]{1,0:T(8,128)(2,1)S(1)}, bf16[96,768]{1,0:T(8,128)(2,1)S(1)}, u32[]{:S(2)}, u32[]{:S(2)}) collective-permute-start(bf16[96,768]{1,0:T(8,128)(2,1)S(1)} %constant_dynamic-update-slice_fusion.refs_3_), channel_id=1, source_target_pairs={{0,5},{1,4},{2,7},{3,6},{4,1},{5,0},{6,3},{7,2},{8,13},{9,12},{10,... | collective-permute-start | bytes 442376 | tf_op jit(solution)/shard_map/ppermute | solution.py:811
  34.2 8.7 %collective-permute-start.8 = (bf16[96,768]{1,0:T(8,128)(2,1)S(1)}, bf16[96,768]{1,0:T(8,128)(2,1)S(1)}, u32[]{:S(2)}, u32[]{:S(2)}) collective-permute-start(bf16[96,768]{1,0:T(8,128)(2,1)S(1)} %constant_dynamic-update-slice_fusion.refs_3_), channel_id=1, source_target_pairs={{0,2},{1,3},{2,0},{3,1},{4,6},{5,7},{6,4},{7,5},{8,10},{9,11},{10,... | collective-permute-start | bytes 442376 | tf_op jit(solution)/shard_map/ppermute | solution.py:811
  37.5 5.5 %collective-permute-start.9 = (bf16[96,768]{1,0:T(8,128)(2,1)S(1)}, bf16[96,768]{1,0:T(8,128)(2,1)S(1)}, u32[]{:S(2)}, u32[]{:S(2)}) collective-permute-start(bf16[96,768]{1,0:T(8,128)(2,1)S(1)} %collective-permute-done.5.refs_4_), channel_id=1, source_target_pairs={{0,2},{1,3},{2,0},{3,1},{4,6},{5,7},{6,4},{7,5},{8,10},{9,11},{10,... | collective-permute-start | bytes 442376 | tf_op jit(solution)/shard_map/ppermute | solution.py:811
  40.5 2.5 %collective-permute-start.10 = (bf16[96,768]{1,0:T(8,128)(2,1)S(1)}, bf16[96,768]{1,0:T(8,128)(2,1)S(1)}, u32[]{:S(2)}, u32[]{:S(2)}) collective-permute-start(bf16[96,768]{1,0:T(8,128)(2,1)S(1)} %collective-permute-done.6.refs_5_), channel_id=1, source_target_pairs={{0,2},{1,3},{2,0},{3,1},{4,6},{5,7},{6,4},{7,5},{8,10},{9,11},{10,... | collective-permute-start | bytes 442376 | tf_op jit(solution)/shard_map/ppermute | solution.py:811
  40.5 2.5 %collective-permute-start.11 = (bf16[96,768]{1,0:T(8,128)(2,1)S(1)}, bf16[96,768]{1,0:T(8,128)(2,1)S(1)}, u32[]{:S(2)}, u32[]{:S(2)}) collective-permute-start(bf16[96,768]{1,0:T(8,128)(2,1)S(1)} %collective-permute-done.7.refs_6_), channel_id=1, source_target_pairs={{0,2},{1,3},{2,0},{3,1},{4,6},{5,7},{6,4},{7,5},{8,10},{9,11},{10,... | collective-permute-start | bytes 442376 | tf_op jit(solution)/shard_map/ppermute | solution.py:811
  49.3 13.1 %collective-permute-start.12 = (bf16[512,384]{1,0:T(8,128)(2,1)}, bf16[512,384]{1,0:T(8,128)(2,1)S(1)}, u32[]{:S(2)}, u32[]{:S(2)}) collective-permute-start(bf16[512,384]{1,0:T(8,128)(2,1)} %get-tuple-element.84.refs_0_), channel_id=1, source_target_pairs={{0,4},{1,5},{2,3},{3,2},{4,0},{5,1},{6,7},{7,6},{8,12},{9,13},{10,... | collective-permute-start | bytes 1179656 | tf_op jit(solution)/shard_map/ppermute | solution.py:811
  50.1 14.6 %collective-permute-start.13 = (bf16[512,384]{1,0:T(8,128)(2,1)}, bf16[512,384]{1,0:T(8,128)(2,1)S(1)}, u32[]{:S(2)}, u32[]{:S(2)}) collective-permute-start(bf16[512,384]{1,0:T(8,128)(2,1)} %get-tuple-element.84.refs_0_), channel_id=1, source_target_pairs={{0,1},{1,0},{2,6},{3,7},{4,5},{5,4},{6,2},{7,3},{8,9},{9,8},{10,14... | collective-permute-start | bytes 1179656 | tf_op jit(solution)/shard_map/ppermute | solution.py:811
  62.4 9.7 %collective-permute-start.14 = (bf16[512,384]{1,0:T(8,128)(2,1)S(1)}, bf16[512,384]{1,0:T(8,128)(2,1)S(1)}, u32[]{:S(2)}, u32[]{:S(2)}) collective-permute-start(bf16[512,384]{1,0:T(8,128)(2,1)S(1)} %collective-permute-done.12.refs_1_), channel_id=1, source_target_pairs={{0,1},{1,0},{2,6},{3,7},{4,5},{5,4},{6,2},{7,3},{8,9},{9,8},{10,14... | collective-permute-start | bytes 1179656 | tf_op jit(solution)/shard_map/ppermute | solution.py:811
  64.2 7.9 %collective-permute-start.15 = (bf16[512,384]{1,0:T(8,128)(2,1)}, bf16[512,384]{1,0:T(8,128)(2,1)S(1)}, u32[]{:S(2)}, u32[]{:S(2)}) collective-permute-start(bf16[512,384]{1,0:T(8,128)(2,1)} %get-tuple-element.84.refs_0_), channel_id=1, source_target_pairs={{0,2},{1,3},{2,0},{3,1},{4,6},{5,7},{6,4},{7,5},{8,10},{9,11},{10,... | collective-permute-start | bytes 1179656 | tf_op jit(solution)/shard_map/ppermute | solution.py:811
  64.2 8.0 %collective-permute-start.16 = (bf16[512,384]{1,0:T(8,128)(2,1)S(1)}, bf16[512,384]{1,0:T(8,128)(2,1)S(1)}, u32[]{:S(2)}, u32[]{:S(2)}) collective-permute-start(bf16[512,384]{1,0:T(8,128)(2,1)S(1)} %collective-permute-done.12.refs_1_), channel_id=1, source_target_pairs={{0,2},{1,3},{2,0},{3,1},{4,6},{5,7},{6,4},{7,5},{8,10},{9,11},{10,... | collective-permute-start | bytes 1179656 | tf_op jit(solution)/shard_map/ppermute | solution.py:811
  64.7 7.5 %collective-permute-start.17 = (bf16[512,384]{1,0:T(8,128)(2,1)S(1)}, bf16[512,384]{1,0:T(8,128)(2,1)S(1)}, u32[]{:S(2)}, u32[]{:S(2)}) collective-permute-start(bf16[512,384]{1,0:T(8,128)(2,1)S(1)} %collective-permute-done.13.refs_2_), channel_id=1, source_target_pairs={{0,2},{1,3},{2,0},{3,1},{4,6},{5,7},{6,4},{7,5},{8,10},{9,11},{10,... | collective-permute-start | bytes 1179656 | tf_op jit(solution)/shard_map/ppermute | solution.py:811
  89.5 18.4 %collective-permute-start.19 = (bf16[128,256]{1,0:T(8,128)(2,1)}, bf16[128,256]{1,0:T(8,128)(2,1)S(1)}, u32[]{:S(2)}, u32[]{:S(2)}) collective-permute-start(bf16[128,256]{1,0:T(8,128)(2,1)} %get-tuple-element.88), channel_id=1, source_target_pairs={{0,8},{1,9},{2,10},{3,11},{4,12},{5,13},{6,14},{7,15},{8,0},{9,1},... | collective-permute-start | bytes 196616 | tf_op jit(solution)/shard_map/ppermute | solution.py:811
  90.5 17.4 %collective-permute-start.20 = (bf16[128,256]{1,0:T(8,128)(2,1)}, bf16[128,256]{1,0:T(8,128)(2,1)S(1)}, u32[]{:S(2)}, u32[]{:S(2)}) collective-permute-start(bf16[128,256]{1,0:T(8,128)(2,1)} %get-tuple-element.89), channel_id=1, source_target_pairs={{0,16},{1,17},{2,18},{3,19},{4,20},{5,21},{6,22},{7,23},{8,24},{9,... | collective-permute-start | bytes 196616 | tf_op jit(solution)/shard_map/ppermute | solution.py:811
  92.2 15.8 %collective-permute-start.21 = (bf16[128,256]{1,0:T(8,128)(2,1)}, bf16[128,256]{1,0:T(8,128)(2,1)S(1)}, u32[]{:S(2)}, u32[]{:S(2)}) collective-permute-start(bf16[128,256]{1,0:T(8,128)(2,1)} %get-tuple-element.90), channel_id=1, source_target_pairs={{0,24},{1,25},{2,26},{3,27},{4,28},{5,29},{6,30},{7,31},{8,16},{9,... | collective-permute-start | bytes 196616 | tf_op jit(solution)/shard_map/ppermute | solution.py:811
  122.3 7.0 %collective-permute-start.22 = (bf16[96,256]{1,0:T(8,128)(2,1)}, bf16[96,256]{1,0:T(8,128)(2,1)S(1)}, u32[]{:S(2)}, u32[]{:S(2)}) collective-permute-start(bf16[96,256]{1,0:T(8,128)(2,1)} %get-tuple-element.118), channel_id=1, source_target_pairs={{0,8},{1,9},{2,10},{3,11},{4,12},{5,13},{6,14},{7,15},{8,0},{9,1},... | collective-permute-start | bytes 147464 | tf_op jit(solution)/shard_map/ppermute | solution.py:811
  122.3 7.9 %collective-permute-start.23 = (bf16[96,256]{1,0:T(8,128)(2,1)}, bf16[96,256]{1,0:T(8,128)(2,1)S(1)}, u32[]{:S(2)}, u32[]{:S(2)}) collective-permute-start(bf16[96,256]{1,0:T(8,128)(2,1)} %get-tuple-element.119), channel_id=1, source_target_pairs={{0,16},{1,17},{2,18},{3,19},{4,20},{5,21},{6,22},{7,23},{8,24},{9,... | collective-permute-start | bytes 147464 | tf_op jit(solution)/shard_map/ppermute | solution.py:811
  124.3 6.2 %collective-permute-start.24 = (bf16[96,256]{1,0:T(8,128)(2,1)}, bf16[96,256]{1,0:T(8,128)(2,1)S(1)}, u32[]{:S(2)}, u32[]{:S(2)}) collective-permute-start(bf16[96,256]{1,0:T(8,128)(2,1)} %get-tuple-element.120), channel_id=1, source_target_pairs={{0,24},{1,25},{2,26},{3,27},{4,28},{5,29},{6,30},{7,31},{8,16},{9,... | collective-permute-start | bytes 147464 | tf_op jit(solution)/shard_map/ppermute | solution.py:811
  126.7 20.2 %collective-permute-start.27 = (bf16[512,256]{1,0:T(8,128)(2,1)S(1)}, bf16[512,256]{1,0:T(8,128)(2,1)S(1)}, u32[]{:S(2)}, u32[]{:S(2)}) collective-permute-start(bf16[512,256]{1,0:T(8,128)(2,1)S(1)} %copy-done.2), channel_id=1, source_target_pairs={{0,4},{1,5},{2,3},{3,2},{4,0},{5,1},{6,7},{7,6},{8,12},{9,13},{10,... | collective-permute-start | bytes 786440 | tf_op jit(solution)/shard_map/ppermute | solution.py:811
  127.8 19.3 %collective-permute-start.28 = (bf16[512,256]{1,0:T(8,128)(2,1)S(1)}, bf16[512,256]{1,0:T(8,128)(2,1)S(1)}, u32[]{:S(2)}, u32[]{:S(2)}) collective-permute-start(bf16[512,256]{1,0:T(8,128)(2,1)S(1)} %copy-done.2), channel_id=1, source_target_pairs={{0,1},{1,0},{2,6},{3,7},{4,5},{5,4},{6,2},{7,3},{8,9},{9,8},{10,14... | collective-permute-start | bytes 786440 | tf_op jit(solution)/shard_map/ppermute | solution.py:811
  129.2 19.4 %collective-permute-start.29 = (bf16[512,256]{1,0:T(8,128)(2,1)S(1)}, bf16[512,256]{1,0:T(8,128)(2,1)S(1)}, u32[]{:S(2)}, u32[]{:S(2)}) collective-permute-start(bf16[512,256]{1,0:T(8,128)(2,1)S(1)} %copy-done.2), channel_id=1, source_target_pairs={{0,5},{1,4},{2,7},{3,6},{4,1},{5,0},{6,3},{7,2},{8,13},{9,12},{10,... | collective-permute-start | bytes 786440 | tf_op jit(solution)/shard_map/ppermute | solution.py:811
  133.8 13.7 %collective-permute-start.25 = (bf16[512,256]{1,0:T(8,128)(2,1)}, bf16[512,256]{1,0:T(8,128)(2,1)S(1)}, u32[]{:S(2)}, u32[]{:S(2)}) collective-permute-start(bf16[512,256]{1,0:T(8,128)(2,1)} %delta.1.g_ref.refs_11_), channel_id=1, source_target_pairs={{0,4},{1,5},{2,3},{3,2},{4,0},{5,1},{6,7},{7,6},{8,12},{9,13},{10,... | collective-permute-start | bytes 786440 | tf_op jit(solution)/shard_map/ppermute | solution.py:811
  135.2 12.5 %collective-permute-start.26 = (bf16[512,256]{1,0:T(8,128)(2,1)}, bf16[512,256]{1,0:T(8,128)(2,1)S(1)}, u32[]{:S(2)}, u32[]{:S(2)}) collective-permute-start(bf16[512,256]{1,0:T(8,128)(2,1)} %delta.1.g_ref.refs_11_), channel_id=1, source_target_pairs={{0,1},{1,0},{2,6},{3,7},{4,5},{5,4},{6,2},{7,3},{8,9},{9,8},{10,14... | collective-permute-start | bytes 786440 | tf_op jit(solution)/shard_map/ppermute | solution.py:811
  147.6 6.4 %collective-permute-start.34 = (bf16[512,256]{1,0:T(8,128)(2,1)S(1)}, bf16[512,256]{1,0:T(8,128)(2,1)S(1)}, u32[]{:S(2)}, u32[]{:S(2)}) collective-permute-start(bf16[512,256]{1,0:T(8,128)(2,1)S(1)} %collective-permute-done.25.refs_12_), channel_id=1, source_target_pairs={{0,1},{1,0},{2,6},{3,7},{4,5},{5,4},{6,2},{7,3},{8,9},{9,8},{10,14... | collective-permute-start | bytes 786440 | tf_op jit(solution)/shard_map/ppermute | solution.py:811
  148.6 5.4 %collective-permute-start.33 = (bf16[512,256]{1,0:T(8,128)(2,1)S(1)}, bf16[512,256]{1,0:T(8,128)(2,1)S(1)}, u32[]{:S(2)}, u32[]{:S(2)}) collective-permute-start(bf16[512,256]{1,0:T(8,128)(2,1)S(1)} %collective-permute-done.29.refs_6_), channel_id=1, source_target_pairs={{0,2},{1,3},{2,0},{3,1},{4,6},{5,7},{6,4},{7,5},{8,10},{9,11},{10,... | collective-permute-start | bytes 786440 | tf_op jit(solution)/shard_map/ppermute | solution.py:811
  148.7 5.4 %collective-permute-start.36 = (bf16[512,256]{1,0:T(8,128)(2,1)S(1)}, bf16[512,256]{1,0:T(8,128)(2,1)S(1)}, u32[]{:S(2)}, u32[]{:S(2)}) collective-permute-start(bf16[512,256]{1,0:T(8,128)(2,1)S(1)} %collective-permute-done.25.refs_12_), channel_id=1, source_target_pairs={{0,2},{1,3},{2,0},{3,1},{4,6},{5,7},{6,4},{7,5},{8,10},{9,11},{10,... | collective-permute-start | bytes 786440 | tf_op jit(solution)/shard_map/ppermute | solution.py:811
  149.2 4.9 %collective-permute-start.35 = (bf16[512,256]{1,0:T(8,128)(2,1)S(1)}, bf16[512,256]{1,0:T(8,128)(2,1)S(1)}, u32[]{:S(2)}, u32[]{:S(2)}) collective-permute-start(bf16[512,256]{1,0:T(8,128)(2,1)S(1)} %copy-done.4), channel_id=1, source_target_pairs={{0,2},{1,3},{2,0},{3,1},{4,6},{5,7},{6,4},{7,5},{8,10},{9,11},{10,... | collective-permute-start | bytes 786440 | tf_op jit(solution)/shard_map/ppermute | solution.py:811
  149.3 4.8 %collective-permute-start.37 = (bf16[512,256]{1,0:T(8,128)(2,1)S(1)}, bf16[512,256]{1,0:T(8,128)(2,1)S(1)}, u32[]{:S(2)}, u32[]{:S(2)}) collective-permute-start(bf16[512,256]{1,0:T(8,128)(2,1)S(1)} %collective-permute-done.26.refs_13_), channel_id=1, source_target_pairs={{0,2},{1,3},{2,0},{3,1},{4,6},{5,7},{6,4},{7,5},{8,10},{9,11},{10,... | collective-permute-start | bytes 786440 | tf_op jit(solution)/shard_map/ppermute | solution.py:811
  178.9 13.6 %collective-permute-start.39 = (bf16[256,768]{1,0:T(8,128)(2,1)}, bf16[256,768]{1,0:T(8,128)(2,1)S(1)}, u32[]{:S(2)}, u32[]{:S(2)}) collective-permute-start(bf16[256,768]{1,0:T(8,128)(2,1)} %get-tuple-element.133), channel_id=1, source_target_pairs={{0,8},{1,9},{2,10},{3,11},{4,12},{5,13},{6,14},{7,15},{8,0},{9,1},... | collective-permute-start | bytes 1179656 | tf_op jit(solution)/shard_map/ppermute | solution.py:811
  181.8 5.7 %collective-permute-start.44 = (bf16[40,768]{1,0:T(8,128)(2,1)S(1)}, bf16[40,768]{1,0:T(8,128)(2,1)S(1)}, u32[]{:S(2)}, u32[]{:S(2)}) collective-permute-start(bf16[40,768]{1,0:T(8,128)(2,1)S(1)} %get-tuple-element.151), channel_id=1, source_target_pairs={{0,5},{1,4},{2,7},{3,6},{4,1},{5,0},{6,3},{7,2},{8,13},{9,12},{10,... | collective-permute-start | bytes 184328 | tf_op jit(solution)/shard_map/ppermute | solution.py:811
  181.9 5.6 %collective-permute-start.43 = (bf16[40,768]{1,0:T(8,128)(2,1)S(1)}, bf16[40,768]{1,0:T(8,128)(2,1)S(1)}, u32[]{:S(2)}, u32[]{:S(2)}) collective-permute-start(bf16[40,768]{1,0:T(8,128)(2,1)S(1)} %get-tuple-element.152), channel_id=1, source_target_pairs={{0,4},{1,5},{2,6},{3,7},{4,0},{5,1},{6,2},{7,3},{8,12},{9,13},{10,... | collective-permute-start | bytes 184328 | tf_op jit(solution)/shard_map/ppermute | solution.py:811
  181.9 6.2 %collective-permute-start.42 = (bf16[40,768]{1,0:T(8,128)(2,1)S(1)}, bf16[40,768]{1,0:T(8,128)(2,1)S(1)}, u32[]{:S(2)}, u32[]{:S(2)}) collective-permute-start(bf16[40,768]{1,0:T(8,128)(2,1)S(1)} %get-tuple-element.150), channel_id=1, source_target_pairs={{0,1},{1,0},{2,3},{3,2},{4,5},{5,4},{6,7},{7,6},{8,9},{9,8},{10,11... | collective-permute-start | bytes 184328 | tf_op jit(solution)/shard_map/ppermute | solution.py:811
  188.1 6.2 %collective-permute-start.47 = (bf16[40,768]{1,0:T(8,128)(2,1)S(1)}, bf16[40,768]{1,0:T(8,128)(2,1)S(1)}, u32[]{:S(2)}, u32[]{:S(2)}) collective-permute-start(bf16[40,768]{1,0:T(8,128)(2,1)S(1)} %fusion.3), channel_id=1, source_target_pairs={{0,24},{1,25},{2,26},{3,27},{4,28},{5,29},{6,30},{7,31},{8,16},{9,... | collective-permute-start | bytes 184328 | tf_op jit(solution)/shard_map/ppermute | solution.py:811
  190.5 10.2 %collective-permute-start.46 = (bf16[40,768]{1,0:T(8,128)(2,1)S(1)}, bf16[40,768]{1,0:T(8,128)(2,1)S(1)}, u32[]{:S(2)}, u32[]{:S(2)}) collective-permute-start(bf16[40,768]{1,0:T(8,128)(2,1)S(1)} %fusion.3), channel_id=1, source_target_pairs={{0,16},{1,17},{2,18},{3,19},{4,20},{5,21},{6,22},{7,23},{8,24},{9,... | collective-permute-start | bytes 184328 | tf_op jit(solution)/shard_map/ppermute | solution.py:811
  190.5 10.2 %collective-permute-start.45 = (bf16[40,768]{1,0:T(8,128)(2,1)S(1)}, bf16[40,768]{1,0:T(8,128)(2,1)S(1)}, u32[]{:S(2)}, u32[]{:S(2)}) collective-permute-start(bf16[40,768]{1,0:T(8,128)(2,1)S(1)} %fusion.3), channel_id=1, source_target_pairs={{0,8},{1,9},{2,10},{3,11},{4,12},{5,13},{6,14},{7,15},{8,0},{9,1},... | collective-permute-start | bytes 184328 | tf_op jit(solution)/shard_map/ppermute | solution.py:811
  192.7 19.2 %collective-permute-start.40 = (bf16[128,768]{1,0:T(8,128)(2,1)S(1)}, bf16[128,768]{1,0:T(8,128)(2,1)S(1)}, u32[]{:S(2)}, u32[]{:S(2)}) collective-permute-start(bf16[128,768]{1,0:T(8,128)(2,1)S(1)} %slice.48), channel_id=1, source_target_pairs={{0,16},{1,17},{2,18},{3,19},{4,20},{5,21},{6,22},{7,23},{8,24},{9,... | collective-permute-start | bytes 589832 | tf_op jit(solution)/shard_map/ppermute | solution.py:811
  200.8 4.3 %collective-permute-start.48 = (bf16[40,768]{1,0:T(8,128)(2,1)S(1)}, bf16[40,768]{1,0:T(8,128)(2,1)S(1)}, u32[]{:S(2)}, u32[]{:S(2)}) collective-permute-start(bf16[40,768]{1,0:T(8,128)(2,1)S(1)} %add_convert_fusion.refs_0_), channel_id=1, source_target_pairs={{0,1},{1,0},{2,3},{3,2},{4,5},{5,4},{6,7},{7,6},{8,9},{9,8},{10,11... | collective-permute-start | bytes 184328 | tf_op jit(solution)/shard_map/ppermute | solution.py:811
  202.7 4.2 %collective-permute-start.49 = (bf16[40,768]{1,0:T(8,128)(2,1)S(1)}, bf16[40,768]{1,0:T(8,128)(2,1)S(1)}, u32[]{:S(2)}, u32[]{:S(2)}) collective-permute-start(bf16[40,768]{1,0:T(8,128)(2,1)S(1)} %add_convert_fusion.refs_0_), channel_id=1, source_target_pairs={{0,4},{1,5},{2,6},{3,7},{4,0},{5,1},{6,2},{7,3},{8,12},{9,13},{10,... | collective-permute-start | bytes 184328 | tf_op jit(solution)/shard_map/ppermute | solution.py:811
  202.7 5.1 %collective-permute-start.50 = (bf16[40,768]{1,0:T(8,128)(2,1)S(1)}, bf16[40,768]{1,0:T(8,128)(2,1)S(1)}, u32[]{:S(2)}, u32[]{:S(2)}) collective-permute-start(bf16[40,768]{1,0:T(8,128)(2,1)S(1)} %add_convert_fusion.refs_0_), channel_id=1, source_target_pairs={{0,5},{1,4},{2,7},{3,6},{4,1},{5,0},{6,3},{7,2},{8,13},{9,12},{10,... | collective-permute-start | bytes 184328 | tf_op jit(solution)/shard_map/ppermute | solution.py:811
  204.3 3.5 %collective-permute-start.51 = (bf16[40,768]{1,0:T(8,128)(2,1)S(1)}, bf16[40,768]{1,0:T(8,128)(2,1)S(1)}, u32[]{:S(2)}, u32[]{:S(2)}) collective-permute-start(bf16[40,768]{1,0:T(8,128)(2,1)S(1)} %add_convert_fusion.refs_0_), channel_id=1, source_target_pairs={{0,2},{1,3},{2,0},{3,1},{4,6},{5,7},{6,4},{7,5},{8,10},{9,11},{10,... | collective-permute-start | bytes 184328 | tf_op jit(solution)/shard_map/ppermute | solution.py:811
  205.1 2.8 %collective-permute-start.52 = (bf16[40,768]{1,0:T(8,128)(2,1)S(1)}, bf16[40,768]{1,0:T(8,128)(2,1)S(1)}, u32[]{:S(2)}, u32[]{:S(2)}) collective-permute-start(bf16[40,768]{1,0:T(8,128)(2,1)S(1)} %collective-permute-done.48.refs_1_), channel_id=1, source_target_pairs={{0,2},{1,3},{2,0},{3,1},{4,6},{5,7},{6,4},{7,5},{8,10},{9,11},{10,... | collective-permute-start | bytes 184328 | tf_op jit(solution)/shard_map/ppermute | solution.py:811
  (62 other events, 351.0 us)
Sparse Core Ops, SparseCore 0:
  10.9 96.9 all-gather.1
where the time goes:
time: 220 us
  Pallas kernels  80.6 us (37%)
  waiting for transfers between devices  61.5 us (28%)
  starting transfers between devices  51.5 us (23%)
  between operations  16.1 us (7%)
  local copies, waits for them, and re-layouts  5.59 us (3%)
  other arithmetic  4.33 us (2%)
    ppermute x55, starting transfers between devices, send(): lax.ppermute(value, AXES, [(j, j ^ (odd if j >> 1 & 1 else even)) for j i...  51.5 us
    ppermute x55, waiting for transfers between devices, send(): lax.ppermute(value, AXES, [(j, j ^ (odd if j >> 1 & 1 else even)) for j i...  50.7 us
    pallas_call x1, Pallas kernels, shards(): pl.pallas_call(functools.partial(far_kernel, fast), in_specs=[SMEM, SMEM]...  22.6 us
    pallas_call x1, Pallas kernels, shards(): pl.pallas_call(functools.partial(attend_kernel, fast), in_specs=[SMEM, SM...  14.9 us
    pallas_call x1, Pallas kernels, shards(): pl.pallas_call(middle, in_specs=[SMEM] + [VMEM] * 6 + [ANY] + [VMEM] * (c...  13.7 us
    all_gather x1, waiting for transfers between devices, gather_all(): return lax.all_gather(value, AXES, axis=0, tiled=True)  10.8 us
    pallas_call x1, Pallas kernels, shards(): pl.pallas_call(functools.partial(near_kernel, fast), in_specs=[SMEM, SMEM...  10.5 us
    unnamed x111, local copies, waits for them, and re-layouts  5.54 us
  transfers between devices with their start and end apart: 56, of which 21 were waited for; matrix products, arithmetic and copies ran while one was open for 2% of the time, Pallas kernels for 19%

commit v1 on v0

--- a/solution.py
+++ b/solution.py
@@ -437,9 +437,9 @@
             outer = jnp.concatenate([pair[1] for pair in pairs], axis=0)
 
             def add(c, total):
-                return total + query_side(stack, outer, block_rows(k_ref, c * 8, 8), block_rows(v_ref, c * 8, 8))
-
-            total = lax.fori_loop(0, block_total // 8, add, jnp.zeros((2 * STACK, WIDE), f32), unroll=2)
+                return total + query_side(stack, outer, block_rows(k_ref, c * 16, 16), block_rows(v_ref, c * 16, 16))
+
+            total = lax.fori_loop(0, block_total // 16, add, jnp.zeros((2 * STACK, WIDE), f32), unroll=2)
             put_query(a, 0, total[:STACK])
             put_query(a, 1, total[STACK:])
 

time: 220 us -> 219 us (level)
  transfers between devices with their start and end apart: 56 -> 56, of which waited for: 21 -> 22; matrix products, arithmetic and copies ran while one was open for 2% -> 2% of each run, Pallas kernels for 19% -> 19%
where the time goes in v1:
time: 219 us; the launch traced here: 218 us
  Pallas kernels  79.2 us (36%)
  waiting for transfers between devices  61.4 us (28%)
  starting transfers between devices  51.7 us (24%)
  between operations  16.1 us (7%)
  local copies, waits for them, and re-layouts  5.6 us (3%)
  other arithmetic  4.33 us (2%)
    ppermute x55, starting transfers between devices, send(): lax.ppermute(value, AXES, [(j, j ^ (odd if j >> 1 & 1 else even)) for j i...  51.6 us
    ppermute x55, waiting for transfers between devices, send(): lax.ppermute(value, AXES, [(j, j ^ (odd if j >> 1 & 1 else even)) for j i...  50.6 us
    pallas_call x1, Pallas kernels, shards(): pl.pallas_call(functools.partial(far_kernel, fast), in_specs=[SMEM, SMEM]...  21.7 us
    pallas_call x1, Pallas kernels, shards(): pl.pallas_call(functools.partial(attend_kernel, fast), in_specs=[SMEM, SM...  14.9 us
    pallas_call x1, Pallas kernels, shards(): pl.pallas_call(middle, in_specs=[SMEM] + [VMEM] * 6 + [ANY] + [VMEM] * (c...  13.7 us
    all_gather x1, waiting for transfers between devices, gather_all(): return lax.all_gather(value, AXES, axis=0, tiled=True)  10.8 us
    pallas_call x1, Pallas kernels, shards(): pl.pallas_call(functools.partial(near_kernel, fast), in_specs=[SMEM, SMEM...  9.99 us
    unnamed x111, local copies, waits for them, and re-layouts  5.54 us
  transfers between devices with their start and end apart: 56, of which 22 were waited for; matrix products, arithmetic and copies ran while one was open for 2% of the time, Pallas kernels for 19%

profile of v1, /device:TPU:0, one launch (start us, length us, event | category | flops | bytes accessed | tf_op | source)
XLA Modules:
  0.0 218.3 jit_solution(12532375341326256179)
XLA Ops:
  7.2 2.8 %pack.1 = (bf16[24,6912]{1,0:T(8,128)(2,1)}, bf16[24,768]{1,0:T(8,128)(2,1)}, bf16[24,768]{1,0:T(8,128)(2,1)}, bf16[24,768]{1,0:T(8,128)(2,1)}, bf16[24,768]{1,0:T(8,128)(2,1)}) custom-call(s32[4,3]{1,0:T(4,128)} %rand_ref.1, bf16[24,768]{1,0:T(8,128)(2,1)} %query_ref.1, bf16[24,768]{1,0:T(8,128)(2,1)} %key_ref.1, bf16[24,768]{1,0:T(8,128)(2,1)} %value_ref.1, ...), custom_call_target="tpu_custom_call" | custom-call | tf_op jit(solution)/shard_map/pack/pallas_call | solution.py:854
  10.0 4.1 %collective-permute-start = (bf16[128,768]{1,0:T(8,128)(2,1)}, bf16[128,768]{1,0:T(8,128)(2,1)S(1)}, u32[]{:S(2)}, u32[]{:S(2)}) collective-permute-start(bf16[128,768]{1,0:T(8,128)(2,1)} %refs_0_.4), channel_id=1, source_target_pairs={{0,16},{1,17},{2,18},{3,19},{4,20},{5,21},{6,22},{7,23},{8,24},{9,... | collective-permute-start | bytes 589832 | tf_op jit(solution)/shard_map/ppermute | solution.py:811
  14.1 1.6 collective-permute-start.2
  16.0 2.5 %collective-permute-start.4 = (bf16[24,768]{1,0:T(8,128)(2,1)}, bf16[24,768]{1,0:T(8,128)(2,1)S(1)}, u32[]{:S(2)}, u32[]{:S(2)}) collective-permute-start(bf16[24,768]{1,0:T(8,128)(2,1)} %get-tuple-element.81), channel_id=1, source_target_pairs={{0,24},{1,25},{2,26},{3,27},{4,28},{5,29},{6,30},{7,31},{8,16},{9,... | collective-permute-start | bytes 110600 | tf_op jit(solution)/shard_map/ppermute | solution.py:811
  20.2 6.1 %collective-permute-done.3 = bf16[24,768]{1,0:T(8,128)(2,1)S(1)} collective-permute-done((bf16[24,768]{1,0:T(8,128)(2,1)}, bf16[24,768]{1,0:T(8,128)(2,1)S(1)}, u32[]{:S(2)}, u32[]{:S(2)}) %collective-permute-start.3) | collective-permute-done | bytes 36896 | tf_op jit(solution)/shard_map/ppermute | solution.py:811
  26.4 1.0 pad_maximum_fusion
  27.4 3.2 %collective-permute-start.1 = (bf16[256,768]{1,0:T(8,128)(2,1)S(1)}, bf16[256,768]{1,0:T(8,128)(2,1)S(1)}, u32[]{:S(2)}, u32[]{:S(2)}) collective-permute-start(bf16[256,768]{1,0:T(8,128)(2,1)S(1)} %pad_maximum_fusion), channel_id=1, source_target_pairs={{0,8},{1,9},{2,10},{3,11},{4,12},{5,13},{6,14},{7,15},{8,0},{9,1},... | collective-permute-start | bytes 1179656 | tf_op jit(solution)/shard_map/ppermute | solution.py:811
  30.7 1.5 collective-permute-start.5
  32.2 1.5 collective-permute-start.6
  34.2 3.2 %collective-permute-done.5.refs_4_ = bf16[96,768]{1,0:T(8,128)(2,1)S(1)} collective-permute-done((bf16[96,768]{1,0:T(8,128)(2,1)S(1)}, bf16[96,768]{1,0:T(8,128)(2,1)S(1)}, u32[]{:S(2)}, u32[]{:S(2)}) %collective-permute-start.5) | collective-permute-done | bytes 147488 | tf_op jit(solution)/shard_map/ppermute | solution.py:811
  37.5 3.0 %collective-permute-done.6.refs_5_ = bf16[96,768]{1,0:T(8,128)(2,1)S(1)} collective-permute-done((bf16[96,768]{1,0:T(8,128)(2,1)S(1)}, bf16[96,768]{1,0:T(8,128)(2,1)S(1)}, u32[]{:S(2)}, u32[]{:S(2)}) %collective-permute-start.6) | collective-permute-done | bytes 147488 | tf_op jit(solution)/shard_map/ppermute | solution.py:811
  44.5 4.7 %project.1 = (bf16[768,768]{1,0:T(8,128)(2,1)}, bf16[128,768]{1,0:T(8,128)(2,1)}, bf16[128,768]{1,0:T(8,128)(2,1)}, bf16[512,256]{1,0:T(8,128)(2,1)}, bf16[512,384]{1,0:T(8,128)(2,1)}, /*index=5*/s32[32,128]{1,0:T(8,128)}) custom-call(s32[4]{0:T(128)} %pad_add_fusion.meta_ref, bf16[8,4,16,768]{3,2,1,0:T(8,128)(2,1)} %refs_0_.3, ...), custom_call_target="tpu_custom_call" | custom-call | tf_op jit(solution)/shard_map/project/pallas_call | solution.py:888
  50.1 1.5 collective-permute-start.13
  51.6 3.8 %collect.1.pair_ref = s32[200]{0:T(256)} custom-call(s32[4]{0:T(128)} %pad_add_fusion.meta_ref, s32[32,128]{1,0:T(8,128)} %get-tuple-element.82.rand_ref), custom_call_target="tpu_custom_call" | custom-call | tf_op jit(solution)/shard_map/collect/pallas_call | solution.py:910
  55.4 7.0 %collective-permute-done.12.refs_1_ = bf16[512,384]{1,0:T(8,128)(2,1)S(1)} collective-permute-done((bf16[512,384]{1,0:T(8,128)(2,1)}, bf16[512,384]{1,0:T(8,128)(2,1)S(1)}, u32[]{:S(2)}, u32[]{:S(2)}) %collective-permute-start.12) | collective-permute-done | bytes 393248 | tf_op jit(solution)/shard_map/ppermute | solution.py:811
  62.4 1.8 collective-permute-start.14
  64.8 7.3 %collective-permute-done.14.refs_3_ = bf16[512,384]{1,0:T(8,128)(2,1)S(1)} collective-permute-done((bf16[512,384]{1,0:T(8,128)(2,1)S(1)}, bf16[512,384]{1,0:T(8,128)(2,1)S(1)}, u32[]{:S(2)}, u32[]{:S(2)}) %collective-permute-start.14) | collective-permute-done | bytes 393248 | tf_op jit(solution)/shard_map/ppermute | solution.py:811
  72.2 1.6 collective-permute-done.18.refs_7_
  74.6 14.9 %attend.1 = (bf16[4096,256]{1,0:T(8,128)(2,1)}, bf16[4096,256]{1,0:T(8,128)(2,1)}, bf16[128,256]{1,0:T(8,128)(2,1)}, bf16[128,256]{1,0:T(8,128)(2,1)}, bf16[128,...) custom-call(s32[4]{0:T(128)} %pad_add_fusion.meta_ref, s32[32,128]{1,0:T(8,128)} %get-tuple-element.82.rand_ref, ...), custom_call_target="tpu_custom_call" | custom-call | tf_op jit(solution)/shard_map/attend/pallas_call | solution.py:920
  89.5 1.1 collective-permute-start.19
  90.5 1.6 collective-permute-start.20
  92.2 1.7 collective-permute-start.21
  94.5 2.7 %select.7 = (bf16[16,768]{1,0:T(8,128)(2,1)}, bf16[16,768]{1,0:T(8,128)(2,1)}, bf16[16,768]{1,0:T(8,128)(2,1)}, bf16[16,3072]{1,0:T(8,128)(2,1)}, bf16[16,3072]{1,0:T(8,128)(2,1)}, /*index=5*/bf16[16,768]{1,0:T(8,128)(2,1)}) custom-call(s32[4]{0:T(128)} %pad_add_fusion.meta_ref, bf16[8,4,16,768]{3,2,1,0:T(8,128)(2,1)} %refs_0_.3, ...), custom_call_target="tpu_custom_call" | custom-call | tf_op jit(solution)/shard_map/select/pallas_call | solution.py:933
  97.2 10.8 %all-gather.2.cloned.1.call-done.refs_6_ = bf16[768,6912]{1,0:T(8,128)(2,1)} async-done(((bf16[24,6912]{1,0:T(8,128)(2,1)}), bf16[768,6912]{1,0:T(8,128)(2,1)}) %all-gather.2.cloned.1.call-update) | async-done | bytes 10616848 | tf_op jit(solution)/shard_map/all_gather | solution.py:846
  108.6 13.7 %middle.1 = (bf16[128,768]{1,0:T(8,128)(2,1)}, f32[128,768]{1,0:T(8,128)}, bf16[96,256]{1,0:T(8,128)(2,1)}, bf16[96,256]{1,0:T(8,128)(2,1)}, bf16[96,256]{1,0:T(...) custom-call(s32[4]{0:T(128)} %pad_add_fusion.meta_ref, bf16[128,256]{1,0:T(8,128)(2,1)} %get-tuple-element.86.refs_0_, ...), custom_call_target="tpu_custom_call" | custom-call | tf_op jit(solution)/shard_map/middle/pallas_call | solution.py:958
  122.3 1.9 collective-permute-start.23
  124.3 2.4 %collective-permute-start.24 = (bf16[96,256]{1,0:T(8,128)(2,1)}, bf16[96,256]{1,0:T(8,128)(2,1)S(1)}, u32[]{:S(2)}, u32[]{:S(2)}) collective-permute-start(bf16[96,256]{1,0:T(8,128)(2,1)} %get-tuple-element.120), channel_id=1, source_target_pairs={{0,24},{1,25},{2,26},{3,27},{4,28},{5,29},{6,30},{7,31},{8,16},{9,... | collective-permute-start | bytes 147464 | tf_op jit(solution)/shard_map/ppermute | solution.py:811
  126.7 1.0 collective-permute-start.27
  127.8 1.5 collective-permute-start.28
  131.0 2.8 %delta.1.g_ref.refs_11_ = bf16[512,256]{1,0:T(8,128)(2,1)} custom-call(bf16[96,256]{1,0:T(8,128)(2,1)} %get-tuple-element.117.refs_0_, bf16[96,256]{1,0:T(8,128)(2,1)} %copy-done.47, bf16[96,256]{1,0:T(8,128)(2,1)} %copy-done.48, bf16[96,256]{1,0:T(8,128)(2,1)} %copy-done.49, f32[512,256]{1,0:T(8,128)} %get-tuple-element.121.refs_4_), custom_call_target="tpu_custom_call" | custom-call | tf_op jit(solution)/shard_map/delta/pallas_call | solution.py:981
  133.8 1.4 collective-permute-start.25
  135.2 1.3 collective-permute-start.26
  136.4 10.0 %near.1 = (bf16[512,256]{1,0:T(8,128)(2,1)}, f32[8,4,16,768]{3,2,1,0:T(8,128)}, f32[8,4,16,768]{3,2,1,0:T(8,128)}, f32[8,16,768]{2,1,0:T(8,128)}, f32[8,16,3072]...) custom-call(s32[4]{0:T(128)} %pad_add_fusion.meta_ref, s32[32,128]{1,0:T(8,128)} %get-tuple-element.82.rand_ref, ...), custom_call_target="tpu_custom_call" | custom-call | flops 12000000000 | bytes 8000000 | tf_op jit(solution)/shard_map/near/pallas_call | solution.py:1008
  147.2 1.5 collective-permute-start.34
  149.7 3.9 %collective-permute-done.34.refs_14_ = bf16[512,256]{1,0:T(8,128)(2,1)S(1)} collective-permute-done((bf16[512,256]{1,0:T(8,128)(2,1)S(1)}, bf16[512,256]{1,0:T(8,128)(2,1)S(1)}, u32[]{:S(2)}, u32[]{:S(2)}) %collective-permute-start.34) | collective-permute-done | bytes 262176 | tf_op jit(solution)/shard_map/ppermute | solution.py:811
  153.7 1.5 collective-permute-done.38.refs_18_
  155.8 21.7 %far.1 = (bf16[256,768]{1,0:T(8,128)(2,1)}, bf16[256,768]{1,0:T(8,128)(2,1)}, f32[4,40,768]{2,1,0:T(8,128)}, bf16[4,40,768]{2,1,0:T(8,128)(2,1)}) custom-call(s32[4]{0:T(128)} %pad_add_fusion.meta_ref, s32[200]{0:T(256)} %collect.1.pair_ref, bf16[4096,256]{1,0:T(8,128)(2,1)} %get-tuple-element.114.k_ref, bf16[4096,256]{1,0:T(8,128)(2,1)} %get-tuple-element.115.v_ref, ...), custom_call_target="tpu_custom_call" | custom-call | tf_op jit(solution)/shard_map/far/pallas_call | solution.py:1020
  178.2 1.1 collective-permute-done.41
  179.3 1.1 fusion.4
  180.6 3.4 %collective-permute-start.42 = (bf16[40,768]{1,0:T(8,128)(2,1)S(1)}, bf16[40,768]{1,0:T(8,128)(2,1)S(1)}, u32[]{:S(2)}, u32[]{:S(2)}) collective-permute-start(bf16[40,768]{1,0:T(8,128)(2,1)S(1)} %get-tuple-element.150), channel_id=1, source_target_pairs={{0,1},{1,0},{2,3},{3,2},{4,5},{5,4},{6,7},{7,6},{8,9},{9,8},{10,11... | collective-permute-start | bytes 184328 | tf_op jit(solution)/shard_map/ppermute | solution.py:811
  184.0 2.1 collective-permute-done.44
  186.8 2.3 %collective-permute-start.47 = (bf16[40,768]{1,0:T(8,128)(2,1)S(1)}, bf16[40,768]{1,0:T(8,128)(2,1)S(1)}, u32[]{:S(2)}, u32[]{:S(2)}) collective-permute-start(bf16[40,768]{1,0:T(8,128)(2,1)S(1)} %fusion.3), channel_id=1, source_target_pairs={{0,24},{1,25},{2,26},{3,27},{4,28},{5,29},{6,30},{7,31},{8,16},{9,... | collective-permute-start | bytes 184328 | tf_op jit(solution)/shard_map/ppermute | solution.py:811
  189.1 2.2 collective-permute-start.45
  193.0 6.3 %collective-permute-done.46 = bf16[40,768]{1,0:T(8,128)(2,1)S(1)} collective-permute-done((bf16[40,768]{1,0:T(8,128)(2,1)S(1)}, bf16[40,768]{1,0:T(8,128)(2,1)S(1)}, u32[]{:S(2)}, u32[]{:S(2)}) %collective-permute-start.46) | collective-permute-done | bytes 61472 | tf_op jit(solution)/shard_map/ppermute | solution.py:811
  199.4 2.0 collective-permute-start.48
  201.4 1.6 collective-permute-start.50
  203.7 1.9 collective-permute-done.49.refs_2_
  208.4 2.2 %spread.1 = (f32[8,4,16,768]{3,2,1,0:T(8,128)}, f32[8,4,16,768]{3,2,1,0:T(8,128)}, f32[8,16,768]{2,1,0:T(8,128)}, f32[8,16,3072]{2,1,0:T(8,128)}, f32[8,16,3072]{2,1,0:T(8,128)}, /*index=5*/f32[8,16,768]{2,1,0:T(8,128)}) custom-call(s32[4]{0:T(128)} %pad_add_fusion.meta_ref, ...), custom_call_target="tpu_custom_call", output_to_operand_aliasing={{0}: (9, {}), {1}: (10, {}), {2}: (11, {}), {3}: (12, {}), ... | custom-call | tf_op jit(solution)/shard_map/spread/pallas_call | solution.py:1063
  (201 shorter events, 20.5 us)
Async XLA Ops:
  7.2 100.7 %all-gather.2.cloned.1.call-start = ((), (), s32[]{:S(2)}) async-start(), calls=%async_computation | async-start | bytes 10948608 | tf_op jit(solution)/shard_map/all_gather | solution.py:846
  10.0 16.3 %collective-permute-start = (bf16[128,768]{1,0:T(8,128)(2,1)}, bf16[128,768]{1,0:T(8,128)(2,1)S(1)}, u32[]{:S(2)}, u32[]{:S(2)}) collective-permute-start(bf16[128,768]{1,0:T(8,128)(2,1)} %refs_0_.4), channel_id=1, source_target_pairs={{0,16},{1,17},{2,18},{3,19},{4,20},{5,21},{6,22},{7,23},{8,24},{9,... | collective-permute-start | bytes 589832 | tf_op jit(solution)/shard_map/ppermute | solution.py:811
  14.1 6.1 %collective-permute-start.2 = (bf16[24,768]{1,0:T(8,128)(2,1)}, bf16[24,768]{1,0:T(8,128)(2,1)S(1)}, u32[]{:S(2)}, u32[]{:S(2)}) collective-permute-start(bf16[24,768]{1,0:T(8,128)(2,1)} %get-tuple-element.79), channel_id=1, source_target_pairs={{0,8},{1,9},{2,10},{3,11},{4,12},{5,13},{6,14},{7,15},{8,0},{9,1},... | collective-permute-start | bytes 110600 | tf_op jit(solution)/shard_map/ppermute | solution.py:811
  15.7 10.7 %collective-permute-start.3 = (bf16[24,768]{1,0:T(8,128)(2,1)}, bf16[24,768]{1,0:T(8,128)(2,1)S(1)}, u32[]{:S(2)}, u32[]{:S(2)}) collective-permute-start(bf16[24,768]{1,0:T(8,128)(2,1)} %get-tuple-element.80), channel_id=1, source_target_pairs={{0,16},{1,17},{2,18},{3,19},{4,20},{5,21},{6,22},{7,23},{8,24},{9,... | collective-permute-start | bytes 110600 | tf_op jit(solution)/shard_map/ppermute | solution.py:811
  16.0 14.6 %collective-permute-start.4 = (bf16[24,768]{1,0:T(8,128)(2,1)}, bf16[24,768]{1,0:T(8,128)(2,1)S(1)}, u32[]{:S(2)}, u32[]{:S(2)}) collective-permute-start(bf16[24,768]{1,0:T(8,128)(2,1)} %get-tuple-element.81), channel_id=1, source_target_pairs={{0,24},{1,25},{2,26},{3,27},{4,28},{5,29},{6,30},{7,31},{8,16},{9,... | collective-permute-start | bytes 110600 | tf_op jit(solution)/shard_map/ppermute | solution.py:811
  27.4 15.6 %collective-permute-start.1 = (bf16[256,768]{1,0:T(8,128)(2,1)S(1)}, bf16[256,768]{1,0:T(8,128)(2,1)S(1)}, u32[]{:S(2)}, u32[]{:S(2)}) collective-permute-start(bf16[256,768]{1,0:T(8,128)(2,1)S(1)} %pad_maximum_fusion), channel_id=1, source_target_pairs={{0,8},{1,9},{2,10},{3,11},{4,12},{5,13},{6,14},{7,15},{8,0},{9,1},... | collective-permute-start | bytes 1179656 | tf_op jit(solution)/shard_map/ppermute | solution.py:811
  30.7 6.8 %collective-permute-start.5 = (bf16[96,768]{1,0:T(8,128)(2,1)S(1)}, bf16[96,768]{1,0:T(8,128)(2,1)S(1)}, u32[]{:S(2)}, u32[]{:S(2)}) collective-permute-start(bf16[96,768]{1,0:T(8,128)(2,1)S(1)} %constant_dynamic-update-slice_fusion.refs_3_), channel_id=1, source_target_pairs={{0,4},{1,5},{2,3},{3,2},{4,0},{5,1},{6,7},{7,6},{8,12},{9,13},{10,... | collective-permute-start | bytes 442376 | tf_op jit(solution)/shard_map/ppermute | solution.py:811
  32.2 8.3 %collective-permute-start.6 = (bf16[96,768]{1,0:T(8,128)(2,1)S(1)}, bf16[96,768]{1,0:T(8,128)(2,1)S(1)}, u32[]{:S(2)}, u32[]{:S(2)}) collective-permute-start(bf16[96,768]{1,0:T(8,128)(2,1)S(1)} %constant_dynamic-update-slice_fusion.refs_3_), channel_id=1, source_target_pairs={{0,1},{1,0},{2,6},{3,7},{4,5},{5,4},{6,2},{7,3},{8,9},{9,8},{10,14... | collective-permute-start | bytes 442376 | tf_op jit(solution)/shard_map/ppermute | solution.py:811
  33.7 6.8 %collective-permute-start.7 = (bf16[96,768]{1,0:T(8,128)(2,1)S(1)}, bf16[96,768]{1,0:T(8,128)(2,1)S(1)}, u32[]{:S(2)}, u32[]{:S(2)}) collective-permute-start(bf16[96,768]{1,0:T(8,128)(2,1)S(1)} %constant_dynamic-update-slice_fusion.refs_3_), channel_id=1, source_target_pairs={{0,5},{1,4},{2,7},{3,6},{4,1},{5,0},{6,3},{7,2},{8,13},{9,12},{10,... | collective-permute-start | bytes 442376 | tf_op jit(solution)/shard_map/ppermute | solution.py:811
  34.2 8.7 %collective-permute-start.8 = (bf16[96,768]{1,0:T(8,128)(2,1)S(1)}, bf16[96,768]{1,0:T(8,128)(2,1)S(1)}, u32[]{:S(2)}, u32[]{:S(2)}) collective-permute-start(bf16[96,768]{1,0:T(8,128)(2,1)S(1)} %constant_dynamic-update-slice_fusion.refs_3_), channel_id=1, source_target_pairs={{0,2},{1,3},{2,0},{3,1},{4,6},{5,7},{6,4},{7,5},{8,10},{9,11},{10,... | collective-permute-start | bytes 442376 | tf_op jit(solution)/shard_map/ppermute | solution.py:811
  37.5 5.5 %collective-permute-start.9 = (bf16[96,768]{1,0:T(8,128)(2,1)S(1)}, bf16[96,768]{1,0:T(8,128)(2,1)S(1)}, u32[]{:S(2)}, u32[]{:S(2)}) collective-permute-start(bf16[96,768]{1,0:T(8,128)(2,1)S(1)} %collective-permute-done.5.refs_4_), channel_id=1, source_target_pairs={{0,2},{1,3},{2,0},{3,1},{4,6},{5,7},{6,4},{7,5},{8,10},{9,11},{10,... | collective-permute-start | bytes 442376 | tf_op jit(solution)/shard_map/ppermute | solution.py:811
  40.5 2.5 %collective-permute-start.10 = (bf16[96,768]{1,0:T(8,128)(2,1)S(1)}, bf16[96,768]{1,0:T(8,128)(2,1)S(1)}, u32[]{:S(2)}, u32[]{:S(2)}) collective-permute-start(bf16[96,768]{1,0:T(8,128)(2,1)S(1)} %collective-permute-done.6.refs_5_), channel_id=1, source_target_pairs={{0,2},{1,3},{2,0},{3,1},{4,6},{5,7},{6,4},{7,5},{8,10},{9,11},{10,... | collective-permute-start | bytes 442376 | tf_op jit(solution)/shard_map/ppermute | solution.py:811
  49.3 13.1 %collective-permute-start.12 = (bf16[512,384]{1,0:T(8,128)(2,1)}, bf16[512,384]{1,0:T(8,128)(2,1)S(1)}, u32[]{:S(2)}, u32[]{:S(2)}) collective-permute-start(bf16[512,384]{1,0:T(8,128)(2,1)} %get-tuple-element.84.refs_0_), channel_id=1, source_target_pairs={{0,4},{1,5},{2,3},{3,2},{4,0},{5,1},{6,7},{7,6},{8,12},{9,13},{10,... | collective-permute-start | bytes 1179656 | tf_op jit(solution)/shard_map/ppermute | solution.py:811
  50.1 14.6 %collective-permute-start.13 = (bf16[512,384]{1,0:T(8,128)(2,1)}, bf16[512,384]{1,0:T(8,128)(2,1)S(1)}, u32[]{:S(2)}, u32[]{:S(2)}) collective-permute-start(bf16[512,384]{1,0:T(8,128)(2,1)} %get-tuple-element.84.refs_0_), channel_id=1, source_target_pairs={{0,1},{1,0},{2,6},{3,7},{4,5},{5,4},{6,2},{7,3},{8,9},{9,8},{10,14... | collective-permute-start | bytes 1179656 | tf_op jit(solution)/shard_map/ppermute | solution.py:811
  62.4 9.7 %collective-permute-start.14 = (bf16[512,384]{1,0:T(8,128)(2,1)S(1)}, bf16[512,384]{1,0:T(8,128)(2,1)S(1)}, u32[]{:S(2)}, u32[]{:S(2)}) collective-permute-start(bf16[512,384]{1,0:T(8,128)(2,1)S(1)} %collective-permute-done.12.refs_1_), channel_id=1, source_target_pairs={{0,1},{1,0},{2,6},{3,7},{4,5},{5,4},{6,2},{7,3},{8,9},{9,8},{10,14... | collective-permute-start | bytes 1179656 | tf_op jit(solution)/shard_map/ppermute | solution.py:811
  64.2 7.9 %collective-permute-start.15 = (bf16[512,384]{1,0:T(8,128)(2,1)}, bf16[512,384]{1,0:T(8,128)(2,1)S(1)}, u32[]{:S(2)}, u32[]{:S(2)}) collective-permute-start(bf16[512,384]{1,0:T(8,128)(2,1)} %get-tuple-element.84.refs_0_), channel_id=1, source_target_pairs={{0,2},{1,3},{2,0},{3,1},{4,6},{5,7},{6,4},{7,5},{8,10},{9,11},{10,... | collective-permute-start | bytes 1179656 | tf_op jit(solution)/shard_map/ppermute | solution.py:811
  64.2 8.0 %collective-permute-start.16 = (bf16[512,384]{1,0:T(8,128)(2,1)S(1)}, bf16[512,384]{1,0:T(8,128)(2,1)S(1)}, u32[]{:S(2)}, u32[]{:S(2)}) collective-permute-start(bf16[512,384]{1,0:T(8,128)(2,1)S(1)} %collective-permute-done.12.refs_1_), channel_id=1, source_target_pairs={{0,2},{1,3},{2,0},{3,1},{4,6},{5,7},{6,4},{7,5},{8,10},{9,11},{10,... | collective-permute-start | bytes 1179656 | tf_op jit(solution)/shard_map/ppermute | solution.py:811
  64.7 7.5 %collective-permute-start.17 = (bf16[512,384]{1,0:T(8,128)(2,1)S(1)}, bf16[512,384]{1,0:T(8,128)(2,1)S(1)}, u32[]{:S(2)}, u32[]{:S(2)}) collective-permute-start(bf16[512,384]{1,0:T(8,128)(2,1)S(1)} %collective-permute-done.13.refs_2_), channel_id=1, source_target_pairs={{0,2},{1,3},{2,0},{3,1},{4,6},{5,7},{6,4},{7,5},{8,10},{9,11},{10,... | collective-permute-start | bytes 1179656 | tf_op jit(solution)/shard_map/ppermute | solution.py:811
  89.5 18.4 %collective-permute-start.19 = (bf16[128,256]{1,0:T(8,128)(2,1)}, bf16[128,256]{1,0:T(8,128)(2,1)S(1)}, u32[]{:S(2)}, u32[]{:S(2)}) collective-permute-start(bf16[128,256]{1,0:T(8,128)(2,1)} %get-tuple-element.88), channel_id=1, source_target_pairs={{0,8},{1,9},{2,10},{3,11},{4,12},{5,13},{6,14},{7,15},{8,0},{9,1},... | collective-permute-start | bytes 196616 | tf_op jit(solution)/shard_map/ppermute | solution.py:811
  90.5 17.4 %collective-permute-start.20 = (bf16[128,256]{1,0:T(8,128)(2,1)}, bf16[128,256]{1,0:T(8,128)(2,1)S(1)}, u32[]{:S(2)}, u32[]{:S(2)}) collective-permute-start(bf16[128,256]{1,0:T(8,128)(2,1)} %get-tuple-element.89), channel_id=1, source_target_pairs={{0,16},{1,17},{2,18},{3,19},{4,20},{5,21},{6,22},{7,23},{8,24},{9,... | collective-permute-start | bytes 196616 | tf_op jit(solution)/shard_map/ppermute | solution.py:811
  92.2 15.8 %collective-permute-start.21 = (bf16[128,256]{1,0:T(8,128)(2,1)}, bf16[128,256]{1,0:T(8,128)(2,1)S(1)}, u32[]{:S(2)}, u32[]{:S(2)}) collective-permute-start(bf16[128,256]{1,0:T(8,128)(2,1)} %get-tuple-element.90), channel_id=1, source_target_pairs={{0,24},{1,25},{2,26},{3,27},{4,28},{5,29},{6,30},{7,31},{8,16},{9,... | collective-permute-start | bytes 196616 | tf_op jit(solution)/shard_map/ppermute | solution.py:811
  122.3 7.0 %collective-permute-start.22 = (bf16[96,256]{1,0:T(8,128)(2,1)}, bf16[96,256]{1,0:T(8,128)(2,1)S(1)}, u32[]{:S(2)}, u32[]{:S(2)}) collective-permute-start(bf16[96,256]{1,0:T(8,128)(2,1)} %get-tuple-element.118), channel_id=1, source_target_pairs={{0,8},{1,9},{2,10},{3,11},{4,12},{5,13},{6,14},{7,15},{8,0},{9,1},... | collective-permute-start | bytes 147464 | tf_op jit(solution)/shard_map/ppermute | solution.py:811
  122.3 7.9 %collective-permute-start.23 = (bf16[96,256]{1,0:T(8,128)(2,1)}, bf16[96,256]{1,0:T(8,128)(2,1)S(1)}, u32[]{:S(2)}, u32[]{:S(2)}) collective-permute-start(bf16[96,256]{1,0:T(8,128)(2,1)} %get-tuple-element.119), channel_id=1, source_target_pairs={{0,16},{1,17},{2,18},{3,19},{4,20},{5,21},{6,22},{7,23},{8,24},{9,... | collective-permute-start | bytes 147464 | tf_op jit(solution)/shard_map/ppermute | solution.py:811
  124.3 6.2 %collective-permute-start.24 = (bf16[96,256]{1,0:T(8,128)(2,1)}, bf16[96,256]{1,0:T(8,128)(2,1)S(1)}, u32[]{:S(2)}, u32[]{:S(2)}) collective-permute-start(bf16[96,256]{1,0:T(8,128)(2,1)} %get-tuple-element.120), channel_id=1, source_target_pairs={{0,24},{1,25},{2,26},{3,27},{4,28},{5,29},{6,30},{7,31},{8,16},{9,... | collective-permute-start | bytes 147464 | tf_op jit(solution)/shard_map/ppermute | solution.py:811
  126.7 19.7 %collective-permute-start.27 = (bf16[512,256]{1,0:T(8,128)(2,1)S(1)}, bf16[512,256]{1,0:T(8,128)(2,1)S(1)}, u32[]{:S(2)}, u32[]{:S(2)}) collective-permute-start(bf16[512,256]{1,0:T(8,128)(2,1)S(1)} %copy-done.2), channel_id=1, source_target_pairs={{0,4},{1,5},{2,3},{3,2},{4,0},{5,1},{6,7},{7,6},{8,12},{9,13},{10,... | collective-permute-start | bytes 786440 | tf_op jit(solution)/shard_map/ppermute | solution.py:811
  127.8 18.8 %collective-permute-start.28 = (bf16[512,256]{1,0:T(8,128)(2,1)S(1)}, bf16[512,256]{1,0:T(8,128)(2,1)S(1)}, u32[]{:S(2)}, u32[]{:S(2)}) collective-permute-start(bf16[512,256]{1,0:T(8,128)(2,1)S(1)} %copy-done.2), channel_id=1, source_target_pairs={{0,1},{1,0},{2,6},{3,7},{4,5},{5,4},{6,2},{7,3},{8,9},{9,8},{10,14... | collective-permute-start | bytes 786440 | tf_op jit(solution)/shard_map/ppermute | solution.py:811
  129.2 19.4 %collective-permute-start.29 = (bf16[512,256]{1,0:T(8,128)(2,1)S(1)}, bf16[512,256]{1,0:T(8,128)(2,1)S(1)}, u32[]{:S(2)}, u32[]{:S(2)}) collective-permute-start(bf16[512,256]{1,0:T(8,128)(2,1)S(1)} %copy-done.2), channel_id=1, source_target_pairs={{0,5},{1,4},{2,7},{3,6},{4,1},{5,0},{6,3},{7,2},{8,13},{9,12},{10,... | collective-permute-start | bytes 786440 | tf_op jit(solution)/shard_map/ppermute | solution.py:811
  133.8 13.3 %collective-permute-start.25 = (bf16[512,256]{1,0:T(8,128)(2,1)}, bf16[512,256]{1,0:T(8,128)(2,1)S(1)}, u32[]{:S(2)}, u32[]{:S(2)}) collective-permute-start(bf16[512,256]{1,0:T(8,128)(2,1)} %delta.1.g_ref.refs_11_), channel_id=1, source_target_pairs={{0,4},{1,5},{2,3},{3,2},{4,0},{5,1},{6,7},{7,6},{8,12},{9,13},{10,... | collective-permute-start | bytes 786440 | tf_op jit(solution)/shard_map/ppermute | solution.py:811
  135.2 12.0 %collective-permute-start.26 = (bf16[512,256]{1,0:T(8,128)(2,1)}, bf16[512,256]{1,0:T(8,128)(2,1)S(1)}, u32[]{:S(2)}, u32[]{:S(2)}) collective-permute-start(bf16[512,256]{1,0:T(8,128)(2,1)} %delta.1.g_ref.refs_11_), channel_id=1, source_target_pairs={{0,1},{1,0},{2,6},{3,7},{4,5},{5,4},{6,2},{7,3},{8,9},{9,8},{10,14... | collective-permute-start | bytes 786440 | tf_op jit(solution)/shard_map/ppermute | solution.py:811
  146.6 2.6 %collective-permute-start.31 = (bf16[512,256]{1,0:T(8,128)(2,1)S(1)}, bf16[512,256]{1,0:T(8,128)(2,1)S(1)}, u32[]{:S(2)}, u32[]{:S(2)}) collective-permute-start(bf16[512,256]{1,0:T(8,128)(2,1)S(1)} %collective-permute-done.27.refs_4_), channel_id=1, source_target_pairs={{0,2},{1,3},{2,0},{3,1},{4,6},{5,7},{6,4},{7,5},{8,10},{9,11},{10,... | collective-permute-start | bytes 786440 | tf_op jit(solution)/shard_map/ppermute | solution.py:811
  147.2 6.4 %collective-permute-start.34 = (bf16[512,256]{1,0:T(8,128)(2,1)S(1)}, bf16[512,256]{1,0:T(8,128)(2,1)S(1)}, u32[]{:S(2)}, u32[]{:S(2)}) collective-permute-start(bf16[512,256]{1,0:T(8,128)(2,1)S(1)} %collective-permute-done.25.refs_12_), channel_id=1, source_target_pairs={{0,1},{1,0},{2,6},{3,7},{4,5},{5,4},{6,2},{7,3},{8,9},{9,8},{10,14... | collective-permute-start | bytes 786440 | tf_op jit(solution)/shard_map/ppermute | solution.py:811
  148.6 5.0 %collective-permute-start.33 = (bf16[512,256]{1,0:T(8,128)(2,1)S(1)}, bf16[512,256]{1,0:T(8,128)(2,1)S(1)}, u32[]{:S(2)}, u32[]{:S(2)}) collective-permute-start(bf16[512,256]{1,0:T(8,128)(2,1)S(1)} %collective-permute-done.29.refs_6_), channel_id=1, source_target_pairs={{0,2},{1,3},{2,0},{3,1},{4,6},{5,7},{6,4},{7,5},{8,10},{9,11},{10,... | collective-permute-start | bytes 786440 | tf_op jit(solution)/shard_map/ppermute | solution.py:811
  148.7 5.0 %collective-permute-start.36 = (bf16[512,256]{1,0:T(8,128)(2,1)S(1)}, bf16[512,256]{1,0:T(8,128)(2,1)S(1)}, u32[]{:S(2)}, u32[]{:S(2)}) collective-permute-start(bf16[512,256]{1,0:T(8,128)(2,1)S(1)} %collective-permute-done.25.refs_12_), channel_id=1, source_target_pairs={{0,2},{1,3},{2,0},{3,1},{4,6},{5,7},{6,4},{7,5},{8,10},{9,11},{10,... | collective-permute-start | bytes 786440 | tf_op jit(solution)/shard_map/ppermute | solution.py:811
  149.2 4.5 %collective-permute-start.35 = (bf16[512,256]{1,0:T(8,128)(2,1)S(1)}, bf16[512,256]{1,0:T(8,128)(2,1)S(1)}, u32[]{:S(2)}, u32[]{:S(2)}) collective-permute-start(bf16[512,256]{1,0:T(8,128)(2,1)S(1)} %copy-done.4), channel_id=1, source_target_pairs={{0,2},{1,3},{2,0},{3,1},{4,6},{5,7},{6,4},{7,5},{8,10},{9,11},{10,... | collective-permute-start | bytes 786440 | tf_op jit(solution)/shard_map/ppermute | solution.py:811
  149.3 4.4 %collective-permute-start.37 = (bf16[512,256]{1,0:T(8,128)(2,1)S(1)}, bf16[512,256]{1,0:T(8,128)(2,1)S(1)}, u32[]{:S(2)}, u32[]{:S(2)}) collective-permute-start(bf16[512,256]{1,0:T(8,128)(2,1)S(1)} %collective-permute-done.26.refs_13_), channel_id=1, source_target_pairs={{0,2},{1,3},{2,0},{3,1},{4,6},{5,7},{6,4},{7,5},{8,10},{9,11},{10,... | collective-permute-start | bytes 786440 | tf_op jit(solution)/shard_map/ppermute | solution.py:811
  177.6 13.6 %collective-permute-start.39 = (bf16[256,768]{1,0:T(8,128)(2,1)}, bf16[256,768]{1,0:T(8,128)(2,1)S(1)}, u32[]{:S(2)}, u32[]{:S(2)}) collective-permute-start(bf16[256,768]{1,0:T(8,128)(2,1)} %get-tuple-element.133), channel_id=1, source_target_pairs={{0,8},{1,9},{2,10},{3,11},{4,12},{5,13},{6,14},{7,15},{8,0},{9,1},... | collective-permute-start | bytes 1179656 | tf_op jit(solution)/shard_map/ppermute | solution.py:811
  180.5 5.7 %collective-permute-start.44 = (bf16[40,768]{1,0:T(8,128)(2,1)S(1)}, bf16[40,768]{1,0:T(8,128)(2,1)S(1)}, u32[]{:S(2)}, u32[]{:S(2)}) collective-permute-start(bf16[40,768]{1,0:T(8,128)(2,1)S(1)} %get-tuple-element.151), channel_id=1, source_target_pairs={{0,5},{1,4},{2,7},{3,6},{4,1},{5,0},{6,3},{7,2},{8,13},{9,12},{10,... | collective-permute-start | bytes 184328 | tf_op jit(solution)/shard_map/ppermute | solution.py:811
  180.5 5.6 %collective-permute-start.43 = (bf16[40,768]{1,0:T(8,128)(2,1)S(1)}, bf16[40,768]{1,0:T(8,128)(2,1)S(1)}, u32[]{:S(2)}, u32[]{:S(2)}) collective-permute-start(bf16[40,768]{1,0:T(8,128)(2,1)S(1)} %get-tuple-element.152), channel_id=1, source_target_pairs={{0,4},{1,5},{2,6},{3,7},{4,0},{5,1},{6,2},{7,3},{8,12},{9,13},{10,... | collective-permute-start | bytes 184328 | tf_op jit(solution)/shard_map/ppermute | solution.py:811
  180.6 6.2 %collective-permute-start.42 = (bf16[40,768]{1,0:T(8,128)(2,1)S(1)}, bf16[40,768]{1,0:T(8,128)(2,1)S(1)}, u32[]{:S(2)}, u32[]{:S(2)}) collective-permute-start(bf16[40,768]{1,0:T(8,128)(2,1)S(1)} %get-tuple-element.150), channel_id=1, source_target_pairs={{0,1},{1,0},{2,3},{3,2},{4,5},{5,4},{6,7},{7,6},{8,9},{9,8},{10,11... | collective-permute-start | bytes 184328 | tf_op jit(solution)/shard_map/ppermute | solution.py:811
  186.8 6.2 %collective-permute-start.47 = (bf16[40,768]{1,0:T(8,128)(2,1)S(1)}, bf16[40,768]{1,0:T(8,128)(2,1)S(1)}, u32[]{:S(2)}, u32[]{:S(2)}) collective-permute-start(bf16[40,768]{1,0:T(8,128)(2,1)S(1)} %fusion.3), channel_id=1, source_target_pairs={{0,24},{1,25},{2,26},{3,27},{4,28},{5,29},{6,30},{7,31},{8,16},{9,... | collective-permute-start | bytes 184328 | tf_op jit(solution)/shard_map/ppermute | solution.py:811
  189.1 10.3 %collective-permute-start.46 = (bf16[40,768]{1,0:T(8,128)(2,1)S(1)}, bf16[40,768]{1,0:T(8,128)(2,1)S(1)}, u32[]{:S(2)}, u32[]{:S(2)}) collective-permute-start(bf16[40,768]{1,0:T(8,128)(2,1)S(1)} %fusion.3), channel_id=1, source_target_pairs={{0,16},{1,17},{2,18},{3,19},{4,20},{5,21},{6,22},{7,23},{8,24},{9,... | collective-permute-start | bytes 184328 | tf_op jit(solution)/shard_map/ppermute | solution.py:811
  189.1 10.3 %collective-permute-start.45 = (bf16[40,768]{1,0:T(8,128)(2,1)S(1)}, bf16[40,768]{1,0:T(8,128)(2,1)S(1)}, u32[]{:S(2)}, u32[]{:S(2)}) collective-permute-start(bf16[40,768]{1,0:T(8,128)(2,1)S(1)} %fusion.3), channel_id=1, source_target_pairs={{0,8},{1,9},{2,10},{3,11},{4,12},{5,13},{6,14},{7,15},{8,0},{9,1},... | collective-permute-start | bytes 184328 | tf_op jit(solution)/shard_map/ppermute | solution.py:811
  191.4 19.3 %collective-permute-start.40 = (bf16[128,768]{1,0:T(8,128)(2,1)S(1)}, bf16[128,768]{1,0:T(8,128)(2,1)S(1)}, u32[]{:S(2)}, u32[]{:S(2)}) collective-permute-start(bf16[128,768]{1,0:T(8,128)(2,1)S(1)} %slice.48), channel_id=1, source_target_pairs={{0,16},{1,17},{2,18},{3,19},{4,20},{5,21},{6,22},{7,23},{8,24},{9,... | collective-permute-start | bytes 589832 | tf_op jit(solution)/shard_map/ppermute | solution.py:811
  199.4 4.3 %collective-permute-start.48 = (bf16[40,768]{1,0:T(8,128)(2,1)S(1)}, bf16[40,768]{1,0:T(8,128)(2,1)S(1)}, u32[]{:S(2)}, u32[]{:S(2)}) collective-permute-start(bf16[40,768]{1,0:T(8,128)(2,1)S(1)} %add_convert_fusion.refs_0_), channel_id=1, source_target_pairs={{0,1},{1,0},{2,3},{3,2},{4,5},{5,4},{6,7},{7,6},{8,9},{9,8},{10,11... | collective-permute-start | bytes 184328 | tf_op jit(solution)/shard_map/ppermute | solution.py:811
  201.4 4.2 %collective-permute-start.49 = (bf16[40,768]{1,0:T(8,128)(2,1)S(1)}, bf16[40,768]{1,0:T(8,128)(2,1)S(1)}, u32[]{:S(2)}, u32[]{:S(2)}) collective-permute-start(bf16[40,768]{1,0:T(8,128)(2,1)S(1)} %add_convert_fusion.refs_0_), channel_id=1, source_target_pairs={{0,4},{1,5},{2,6},{3,7},{4,0},{5,1},{6,2},{7,3},{8,12},{9,13},{10,... | collective-permute-start | bytes 184328 | tf_op jit(solution)/shard_map/ppermute | solution.py:811
  201.4 5.1 %collective-permute-start.50 = (bf16[40,768]{1,0:T(8,128)(2,1)S(1)}, bf16[40,768]{1,0:T(8,128)(2,1)S(1)}, u32[]{:S(2)}, u32[]{:S(2)}) collective-permute-start(bf16[40,768]{1,0:T(8,128)(2,1)S(1)} %add_convert_fusion.refs_0_), channel_id=1, source_target_pairs={{0,5},{1,4},{2,7},{3,6},{4,1},{5,0},{6,3},{7,2},{8,13},{9,12},{10,... | collective-permute-start | bytes 184328 | tf_op jit(solution)/shard_map/ppermute | solution.py:811
  203.0 3.6 %collective-permute-start.51 = (bf16[40,768]{1,0:T(8,128)(2,1)S(1)}, bf16[40,768]{1,0:T(8,128)(2,1)S(1)}, u32[]{:S(2)}, u32[]{:S(2)}) collective-permute-start(bf16[40,768]{1,0:T(8,128)(2,1)S(1)} %add_convert_fusion.refs_0_), channel_id=1, source_target_pairs={{0,2},{1,3},{2,0},{3,1},{4,6},{5,7},{6,4},{7,5},{8,10},{9,11},{10,... | collective-permute-start | bytes 184328 | tf_op jit(solution)/shard_map/ppermute | solution.py:811
  203.7 2.9 %collective-permute-start.52 = (bf16[40,768]{1,0:T(8,128)(2,1)S(1)}, bf16[40,768]{1,0:T(8,128)(2,1)S(1)}, u32[]{:S(2)}, u32[]{:S(2)}) collective-permute-start(bf16[40,768]{1,0:T(8,128)(2,1)S(1)} %collective-permute-done.48.refs_1_), channel_id=1, source_target_pairs={{0,2},{1,3},{2,0},{3,1},{4,6},{5,7},{6,4},{7,5},{8,10},{9,11},{10,... | collective-permute-start | bytes 184328 | tf_op jit(solution)/shard_map/ppermute | solution.py:811
  (62 other events, 350.5 us)
Sparse Core Ops, SparseCore 0:
  10.9 96.9 all-gather.1

commit v2 on v1

--- a/solution.py
+++ b/solution.py
@@ -551,10 +551,10 @@
         values = block_rows(v_ref, 0, 2)
 
         def every(step, carry):
-            put(here, key_side(keys, values, [4 * step + k for k in range(4)], None))
+            put(here, key_side(keys, values, [8 * step + k for k in range(8)], None))
             return carry
 
-        lax.fori_loop(0, block_total // 4, every, 0, unroll=4)
+        lax.fori_loop(0, block_total // 8, every, 0, unroll=2)
 
     data = lanes(rows) < SHARE
     for a in range(4):

time: 219 us -> 218 us (level)
  no operation moved by 1% of the time
where the time goes in v2:
time: 218 us
  Pallas kernels  78.7 us (36%)
  waiting for transfers between devices  61.4 us (28%)
  starting transfers between devices  51.7 us (24%)
  between operations  16.1 us (7%)
  local copies, waits for them, and re-layouts  5.6 us (3%)
  other arithmetic  4.33 us (2%)
    ppermute x55, starting transfers between devices, send(): lax.ppermute(value, AXES, [(j, j ^ (odd if j >> 1 & 1 else even)) for j i...  51.6 us
    ppermute x55, waiting for transfers between devices, send(): lax.ppermute(value, AXES, [(j, j ^ (odd if j >> 1 & 1 else even)) for j i...  50.6 us
    pallas_call x1, Pallas kernels, shards(): pl.pallas_call(functools.partial(far_kernel, fast), in_specs=[SMEM, SMEM]...  21.2 us
    pallas_call x1, Pallas kernels, shards(): pl.pallas_call(functools.partial(attend_kernel, fast), in_specs=[SMEM, SM...  14.9 us
    pallas_call x1, Pallas kernels, shards(): pl.pallas_call(middle, in_specs=[SMEM] + [VMEM] * 6 + [ANY] + [VMEM] * (c...  13.7 us
    all_gather x1, waiting for transfers between devices, gather_all(): return lax.all_gather(value, AXES, axis=0, tiled=True)  10.8 us
    pallas_call x1, Pallas kernels, shards(): pl.pallas_call(functools.partial(near_kernel, fast), in_specs=[SMEM, SMEM...  9.99 us
    unnamed x111, local copies, waits for them, and re-layouts  5.54 us
  transfers between devices with their start and end apart: 56, of which 22 were waited for; matrix products, arithmetic and copies ran while one was open for 2% of the time, Pallas kernels for 19%

profile of v2, /device:TPU:0, one launch (start us, length us, event | category | flops | bytes accessed | tf_op | source)
XLA Modules:
  0.0 217.8 jit_solution(13745351239956593968)
XLA Ops:
  7.2 2.8 %pack.1 = (bf16[24,6912]{1,0:T(8,128)(2,1)}, bf16[24,768]{1,0:T(8,128)(2,1)}, bf16[24,768]{1,0:T(8,128)(2,1)}, bf16[24,768]{1,0:T(8,128)(2,1)}, bf16[24,768]{1,0:T(8,128)(2,1)}) custom-call(s32[4,3]{1,0:T(4,128)} %rand_ref.1, bf16[24,768]{1,0:T(8,128)(2,1)} %query_ref.1, bf16[24,768]{1,0:T(8,128)(2,1)} %key_ref.1, bf16[24,768]{1,0:T(8,128)(2,1)} %value_ref.1, ...), custom_call_target="tpu_custom_call" | custom-call | tf_op jit(solution)/shard_map/pack/pallas_call | solution.py:854
  10.0 4.1 %collective-permute-start = (bf16[128,768]{1,0:T(8,128)(2,1)}, bf16[128,768]{1,0:T(8,128)(2,1)S(1)}, u32[]{:S(2)}, u32[]{:S(2)}) collective-permute-start(bf16[128,768]{1,0:T(8,128)(2,1)} %refs_0_.4), channel_id=1, source_target_pairs={{0,16},{1,17},{2,18},{3,19},{4,20},{5,21},{6,22},{7,23},{8,24},{9,... | collective-permute-start | bytes 589832 | tf_op jit(solution)/shard_map/ppermute | solution.py:811
  14.1 1.6 collective-permute-start.2
  16.0 2.5 %collective-permute-start.4 = (bf16[24,768]{1,0:T(8,128)(2,1)}, bf16[24,768]{1,0:T(8,128)(2,1)S(1)}, u32[]{:S(2)}, u32[]{:S(2)}) collective-permute-start(bf16[24,768]{1,0:T(8,128)(2,1)} %get-tuple-element.81), channel_id=1, source_target_pairs={{0,24},{1,25},{2,26},{3,27},{4,28},{5,29},{6,30},{7,31},{8,16},{9,... | collective-permute-start | bytes 110600 | tf_op jit(solution)/shard_map/ppermute | solution.py:811
  20.2 6.1 %collective-permute-done.3 = bf16[24,768]{1,0:T(8,128)(2,1)S(1)} collective-permute-done((bf16[24,768]{1,0:T(8,128)(2,1)}, bf16[24,768]{1,0:T(8,128)(2,1)S(1)}, u32[]{:S(2)}, u32[]{:S(2)}) %collective-permute-start.3) | collective-permute-done | bytes 36896 | tf_op jit(solution)/shard_map/ppermute | solution.py:811
  26.4 1.0 pad_maximum_fusion
  27.4 3.2 %collective-permute-start.1 = (bf16[256,768]{1,0:T(8,128)(2,1)S(1)}, bf16[256,768]{1,0:T(8,128)(2,1)S(1)}, u32[]{:S(2)}, u32[]{:S(2)}) collective-permute-start(bf16[256,768]{1,0:T(8,128)(2,1)S(1)} %pad_maximum_fusion), channel_id=1, source_target_pairs={{0,8},{1,9},{2,10},{3,11},{4,12},{5,13},{6,14},{7,15},{8,0},{9,1},... | collective-permute-start | bytes 1179656 | tf_op jit(solution)/shard_map/ppermute | solution.py:811
  30.7 1.5 collective-permute-start.5
  32.2 1.5 collective-permute-start.6
  34.2 3.2 %collective-permute-done.5.refs_4_ = bf16[96,768]{1,0:T(8,128)(2,1)S(1)} collective-permute-done((bf16[96,768]{1,0:T(8,128)(2,1)S(1)}, bf16[96,768]{1,0:T(8,128)(2,1)S(1)}, u32[]{:S(2)}, u32[]{:S(2)}) %collective-permute-start.5) | collective-permute-done | bytes 147488 | tf_op jit(solution)/shard_map/ppermute | solution.py:811
  37.5 3.0 %collective-permute-done.6.refs_5_ = bf16[96,768]{1,0:T(8,128)(2,1)S(1)} collective-permute-done((bf16[96,768]{1,0:T(8,128)(2,1)S(1)}, bf16[96,768]{1,0:T(8,128)(2,1)S(1)}, u32[]{:S(2)}, u32[]{:S(2)}) %collective-permute-start.6) | collective-permute-done | bytes 147488 | tf_op jit(solution)/shard_map/ppermute | solution.py:811
  44.5 4.7 %project.1 = (bf16[768,768]{1,0:T(8,128)(2,1)}, bf16[128,768]{1,0:T(8,128)(2,1)}, bf16[128,768]{1,0:T(8,128)(2,1)}, bf16[512,256]{1,0:T(8,128)(2,1)}, bf16[512,384]{1,0:T(8,128)(2,1)}, /*index=5*/s32[32,128]{1,0:T(8,128)}) custom-call(s32[4]{0:T(128)} %pad_add_fusion.meta_ref, bf16[8,4,16,768]{3,2,1,0:T(8,128)(2,1)} %refs_0_.3, ...), custom_call_target="tpu_custom_call" | custom-call | tf_op jit(solution)/shard_map/project/pallas_call | solution.py:888
  50.1 1.5 collective-permute-start.13
  51.6 3.8 %collect.1.pair_ref = s32[200]{0:T(256)} custom-call(s32[4]{0:T(128)} %pad_add_fusion.meta_ref, s32[32,128]{1,0:T(8,128)} %get-tuple-element.82.rand_ref), custom_call_target="tpu_custom_call" | custom-call | tf_op jit(solution)/shard_map/collect/pallas_call | solution.py:910
  55.4 7.0 %collective-permute-done.12.refs_1_ = bf16[512,384]{1,0:T(8,128)(2,1)S(1)} collective-permute-done((bf16[512,384]{1,0:T(8,128)(2,1)}, bf16[512,384]{1,0:T(8,128)(2,1)S(1)}, u32[]{:S(2)}, u32[]{:S(2)}) %collective-permute-start.12) | collective-permute-done | bytes 393248 | tf_op jit(solution)/shard_map/ppermute | solution.py:811
  62.4 1.8 collective-permute-start.14
  64.8 7.3 %collective-permute-done.14.refs_3_ = bf16[512,384]{1,0:T(8,128)(2,1)S(1)} collective-permute-done((bf16[512,384]{1,0:T(8,128)(2,1)S(1)}, bf16[512,384]{1,0:T(8,128)(2,1)S(1)}, u32[]{:S(2)}, u32[]{:S(2)}) %collective-permute-start.14) | collective-permute-done | bytes 393248 | tf_op jit(solution)/shard_map/ppermute | solution.py:811
  72.2 1.6 collective-permute-done.18.refs_7_
  74.6 14.9 %attend.1 = (bf16[4096,256]{1,0:T(8,128)(2,1)}, bf16[4096,256]{1,0:T(8,128)(2,1)}, bf16[128,256]{1,0:T(8,128)(2,1)}, bf16[128,256]{1,0:T(8,128)(2,1)}, bf16[128,...) custom-call(s32[4]{0:T(128)} %pad_add_fusion.meta_ref, s32[32,128]{1,0:T(8,128)} %get-tuple-element.82.rand_ref, ...), custom_call_target="tpu_custom_call" | custom-call | tf_op jit(solution)/shard_map/attend/pallas_call | solution.py:920
  89.5 1.1 collective-permute-start.19
  90.5 1.6 collective-permute-start.20
  92.2 1.7 collective-permute-start.21
  94.5 2.7 %select.7 = (bf16[16,768]{1,0:T(8,128)(2,1)}, bf16[16,768]{1,0:T(8,128)(2,1)}, bf16[16,768]{1,0:T(8,128)(2,1)}, bf16[16,3072]{1,0:T(8,128)(2,1)}, bf16[16,3072]{1,0:T(8,128)(2,1)}, /*index=5*/bf16[16,768]{1,0:T(8,128)(2,1)}) custom-call(s32[4]{0:T(128)} %pad_add_fusion.meta_ref, bf16[8,4,16,768]{3,2,1,0:T(8,128)(2,1)} %refs_0_.3, ...), custom_call_target="tpu_custom_call" | custom-call | tf_op jit(solution)/shard_map/select/pallas_call | solution.py:933
  97.2 10.8 %all-gather.2.cloned.1.call-done.refs_6_ = bf16[768,6912]{1,0:T(8,128)(2,1)} async-done(((bf16[24,6912]{1,0:T(8,128)(2,1)}), bf16[768,6912]{1,0:T(8,128)(2,1)}) %all-gather.2.cloned.1.call-update) | async-done | bytes 10616848 | tf_op jit(solution)/shard_map/all_gather | solution.py:846
  108.6 13.7 %middle.1 = (bf16[128,768]{1,0:T(8,128)(2,1)}, f32[128,768]{1,0:T(8,128)}, bf16[96,256]{1,0:T(8,128)(2,1)}, bf16[96,256]{1,0:T(8,128)(2,1)}, bf16[96,256]{1,0:T(...) custom-call(s32[4]{0:T(128)} %pad_add_fusion.meta_ref, bf16[128,256]{1,0:T(8,128)(2,1)} %get-tuple-element.86.refs_0_, ...), custom_call_target="tpu_custom_call" | custom-call | tf_op jit(solution)/shard_map/middle/pallas_call | solution.py:958
  122.3 1.9 collective-permute-start.23
  124.3 2.4 %collective-permute-start.24 = (bf16[96,256]{1,0:T(8,128)(2,1)}, bf16[96,256]{1,0:T(8,128)(2,1)S(1)}, u32[]{:S(2)}, u32[]{:S(2)}) collective-permute-start(bf16[96,256]{1,0:T(8,128)(2,1)} %get-tuple-element.120), channel_id=1, source_target_pairs={{0,24},{1,25},{2,26},{3,27},{4,28},{5,29},{6,30},{7,31},{8,16},{9,... | collective-permute-start | bytes 147464 | tf_op jit(solution)/shard_map/ppermute | solution.py:811
  126.7 1.0 collective-permute-start.27
  127.8 1.5 collective-permute-start.28
  131.0 2.8 %delta.1.g_ref.refs_11_ = bf16[512,256]{1,0:T(8,128)(2,1)} custom-call(bf16[96,256]{1,0:T(8,128)(2,1)} %get-tuple-element.117.refs_0_, bf16[96,256]{1,0:T(8,128)(2,1)} %copy-done.47, bf16[96,256]{1,0:T(8,128)(2,1)} %copy-done.48, bf16[96,256]{1,0:T(8,128)(2,1)} %copy-done.49, f32[512,256]{1,0:T(8,128)} %get-tuple-element.121.refs_4_), custom_call_target="tpu_custom_call" | custom-call | tf_op jit(solution)/shard_map/delta/pallas_call | solution.py:981
  133.8 1.4 collective-permute-start.25
  135.2 1.3 collective-permute-start.26
  136.4 10.0 %near.1 = (bf16[512,256]{1,0:T(8,128)(2,1)}, f32[8,4,16,768]{3,2,1,0:T(8,128)}, f32[8,4,16,768]{3,2,1,0:T(8,128)}, f32[8,16,768]{2,1,0:T(8,128)}, f32[8,16,3072]...) custom-call(s32[4]{0:T(128)} %pad_add_fusion.meta_ref, s32[32,128]{1,0:T(8,128)} %get-tuple-element.82.rand_ref, ...), custom_call_target="tpu_custom_call" | custom-call | flops 12000000000 | bytes 8000000 | tf_op jit(solution)/shard_map/near/pallas_call | solution.py:1008
  147.2 1.5 collective-permute-start.34
  149.7 3.9 %collective-permute-done.34.refs_14_ = bf16[512,256]{1,0:T(8,128)(2,1)S(1)} collective-permute-done((bf16[512,256]{1,0:T(8,128)(2,1)S(1)}, bf16[512,256]{1,0:T(8,128)(2,1)S(1)}, u32[]{:S(2)}, u32[]{:S(2)}) %collective-permute-start.34) | collective-permute-done | bytes 262176 | tf_op jit(solution)/shard_map/ppermute | solution.py:811
  153.7 1.5 collective-permute-done.38.refs_18_
  155.8 21.2 %far.1 = (bf16[256,768]{1,0:T(8,128)(2,1)}, bf16[256,768]{1,0:T(8,128)(2,1)}, f32[4,40,768]{2,1,0:T(8,128)}, bf16[4,40,768]{2,1,0:T(8,128)(2,1)}) custom-call(s32[4]{0:T(128)} %pad_add_fusion.meta_ref, s32[200]{0:T(256)} %collect.1.pair_ref, bf16[4096,256]{1,0:T(8,128)(2,1)} %get-tuple-element.114.k_ref, bf16[4096,256]{1,0:T(8,128)(2,1)} %get-tuple-element.115.v_ref, ...), custom_call_target="tpu_custom_call" | custom-call | tf_op jit(solution)/shard_map/far/pallas_call | solution.py:1020
  177.8 1.1 collective-permute-done.41
  178.9 1.1 fusion.4
  180.1 3.4 %collective-permute-start.42 = (bf16[40,768]{1,0:T(8,128)(2,1)S(1)}, bf16[40,768]{1,0:T(8,128)(2,1)S(1)}, u32[]{:S(2)}, u32[]{:S(2)}) collective-permute-start(bf16[40,768]{1,0:T(8,128)(2,1)S(1)} %get-tuple-element.150), channel_id=1, source_target_pairs={{0,1},{1,0},{2,3},{3,2},{4,5},{5,4},{6,7},{7,6},{8,9},{9,8},{10,11... | collective-permute-start | bytes 184328 | tf_op jit(solution)/shard_map/ppermute | solution.py:811
  183.5 2.1 collective-permute-done.44
  186.4 2.3 %collective-permute-start.47 = (bf16[40,768]{1,0:T(8,128)(2,1)S(1)}, bf16[40,768]{1,0:T(8,128)(2,1)S(1)}, u32[]{:S(2)}, u32[]{:S(2)}) collective-permute-start(bf16[40,768]{1,0:T(8,128)(2,1)S(1)} %fusion.3), channel_id=1, source_target_pairs={{0,24},{1,25},{2,26},{3,27},{4,28},{5,29},{6,30},{7,31},{8,16},{9,... | collective-permute-start | bytes 184328 | tf_op jit(solution)/shard_map/ppermute | solution.py:811
  188.6 2.2 collective-permute-start.45
  192.6 6.3 %collective-permute-done.46 = bf16[40,768]{1,0:T(8,128)(2,1)S(1)} collective-permute-done((bf16[40,768]{1,0:T(8,128)(2,1)S(1)}, bf16[40,768]{1,0:T(8,128)(2,1)S(1)}, u32[]{:S(2)}, u32[]{:S(2)}) %collective-permute-start.46) | collective-permute-done | bytes 61472 | tf_op jit(solution)/shard_map/ppermute | solution.py:811
  198.9 2.0 collective-permute-start.48
  200.9 1.6 collective-permute-start.50
  203.2 1.9 collective-permute-done.49.refs_2_
  207.9 2.2 %spread.1 = (f32[8,4,16,768]{3,2,1,0:T(8,128)}, f32[8,4,16,768]{3,2,1,0:T(8,128)}, f32[8,16,768]{2,1,0:T(8,128)}, f32[8,16,3072]{2,1,0:T(8,128)}, f32[8,16,3072]{2,1,0:T(8,128)}, /*index=5*/f32[8,16,768]{2,1,0:T(8,128)}) custom-call(s32[4]{0:T(128)} %pad_add_fusion.meta_ref, ...), custom_call_target="tpu_custom_call", output_to_operand_aliasing={{0}: (9, {}), {1}: (10, {}), {2}: (11, {}), {3}: (12, {}), ... | custom-call | tf_op jit(solution)/shard_map/spread/pallas_call | solution.py:1063
  (201 shorter events, 20.5 us)
Async XLA Ops:
  7.2 100.7 %all-gather.2.cloned.1.call-start = ((), (), s32[]{:S(2)}) async-start(), calls=%async_computation | async-start | bytes 10948608 | tf_op jit(solution)/shard_map/all_gather | solution.py:846
  10.0 16.3 %collective-permute-start = (bf16[128,768]{1,0:T(8,128)(2,1)}, bf16[128,768]{1,0:T(8,128)(2,1)S(1)}, u32[]{:S(2)}, u32[]{:S(2)}) collective-permute-start(bf16[128,768]{1,0:T(8,128)(2,1)} %refs_0_.4), channel_id=1, source_target_pairs={{0,16},{1,17},{2,18},{3,19},{4,20},{5,21},{6,22},{7,23},{8,24},{9,... | collective-permute-start | bytes 589832 | tf_op jit(solution)/shard_map/ppermute | solution.py:811
  14.1 6.1 %collective-permute-start.2 = (bf16[24,768]{1,0:T(8,128)(2,1)}, bf16[24,768]{1,0:T(8,128)(2,1)S(1)}, u32[]{:S(2)}, u32[]{:S(2)}) collective-permute-start(bf16[24,768]{1,0:T(8,128)(2,1)} %get-tuple-element.79), channel_id=1, source_target_pairs={{0,8},{1,9},{2,10},{3,11},{4,12},{5,13},{6,14},{7,15},{8,0},{9,1},... | collective-permute-start | bytes 110600 | tf_op jit(solution)/shard_map/ppermute | solution.py:811
  15.7 10.7 %collective-permute-start.3 = (bf16[24,768]{1,0:T(8,128)(2,1)}, bf16[24,768]{1,0:T(8,128)(2,1)S(1)}, u32[]{:S(2)}, u32[]{:S(2)}) collective-permute-start(bf16[24,768]{1,0:T(8,128)(2,1)} %get-tuple-element.80), channel_id=1, source_target_pairs={{0,16},{1,17},{2,18},{3,19},{4,20},{5,21},{6,22},{7,23},{8,24},{9,... | collective-permute-start | bytes 110600 | tf_op jit(solution)/shard_map/ppermute | solution.py:811
  16.0 14.6 %collective-permute-start.4 = (bf16[24,768]{1,0:T(8,128)(2,1)}, bf16[24,768]{1,0:T(8,128)(2,1)S(1)}, u32[]{:S(2)}, u32[]{:S(2)}) collective-permute-start(bf16[24,768]{1,0:T(8,128)(2,1)} %get-tuple-element.81), channel_id=1, source_target_pairs={{0,24},{1,25},{2,26},{3,27},{4,28},{5,29},{6,30},{7,31},{8,16},{9,... | collective-permute-start | bytes 110600 | tf_op jit(solution)/shard_map/ppermute | solution.py:811
  27.4 15.6 %collective-permute-start.1 = (bf16[256,768]{1,0:T(8,128)(2,1)S(1)}, bf16[256,768]{1,0:T(8,128)(2,1)S(1)}, u32[]{:S(2)}, u32[]{:S(2)}) collective-permute-start(bf16[256,768]{1,0:T(8,128)(2,1)S(1)} %pad_maximum_fusion), channel_id=1, source_target_pairs={{0,8},{1,9},{2,10},{3,11},{4,12},{5,13},{6,14},{7,15},{8,0},{9,1},... | collective-permute-start | bytes 1179656 | tf_op jit(solution)/shard_map/ppermute | solution.py:811
  30.7 6.8 %collective-permute-start.5 = (bf16[96,768]{1,0:T(8,128)(2,1)S(1)}, bf16[96,768]{1,0:T(8,128)(2,1)S(1)}, u32[]{:S(2)}, u32[]{:S(2)}) collective-permute-start(bf16[96,768]{1,0:T(8,128)(2,1)S(1)} %constant_dynamic-update-slice_fusion.refs_3_), channel_id=1, source_target_pairs={{0,4},{1,5},{2,3},{3,2},{4,0},{5,1},{6,7},{7,6},{8,12},{9,13},{10,... | collective-permute-start | bytes 442376 | tf_op jit(solution)/shard_map/ppermute | solution.py:811
  32.2 8.3 %collective-permute-start.6 = (bf16[96,768]{1,0:T(8,128)(2,1)S(1)}, bf16[96,768]{1,0:T(8,128)(2,1)S(1)}, u32[]{:S(2)}, u32[]{:S(2)}) collective-permute-start(bf16[96,768]{1,0:T(8,128)(2,1)S(1)} %constant_dynamic-update-slice_fusion.refs_3_), channel_id=1, source_target_pairs={{0,1},{1,0},{2,6},{3,7},{4,5},{5,4},{6,2},{7,3},{8,9},{9,8},{10,14... | collective-permute-start | bytes 442376 | tf_op jit(solution)/shard_map/ppermute | solution.py:811
  33.7 6.8 %collective-permute-start.7 = (bf16[96,768]{1,0:T(8,128)(2,1)S(1)}, bf16[96,768]{1,0:T(8,128)(2,1)S(1)}, u32[]{:S(2)}, u32[]{:S(2)}) collective-permute-start(bf16[96,768]{1,0:T(8,128)(2,1)S(1)} %constant_dynamic-update-slice_fusion.refs_3_), channel_id=1, source_target_pairs={{0,5},{1,4},{2,7},{3,6},{4,1},{5,0},{6,3},{7,2},{8,13},{9,12},{10,... | collective-permute-start | bytes 442376 | tf_op jit(solution)/shard_map/ppermute | solution.py:811
  34.2 8.7 %collective-permute-start.8 = (bf16[96,768]{1,0:T(8,128)(2,1)S(1)}, bf16[96,768]{1,0:T(8,128)(2,1)S(1)}, u32[]{:S(2)}, u32[]{:S(2)}) collective-permute-start(bf16[96,768]{1,0:T(8,128)(2,1)S(1)} %constant_dynamic-update-slice_fusion.refs_3_), channel_id=1, source_target_pairs={{0,2},{1,3},{2,0},{3,1},{4,6},{5,7},{6,4},{7,5},{8,10},{9,11},{10,... | collective-permute-start | bytes 442376 | tf_op jit(solution)/shard_map/ppermute | solution.py:811
  37.5 5.5 %collective-permute-start.9 = (bf16[96,768]{1,0:T(8,128)(2,1)S(1)}, bf16[96,768]{1,0:T(8,128)(2,1)S(1)}, u32[]{:S(2)}, u32[]{:S(2)}) collective-permute-start(bf16[96,768]{1,0:T(8,128)(2,1)S(1)} %collective-permute-done.5.refs_4_), channel_id=1, source_target_pairs={{0,2},{1,3},{2,0},{3,1},{4,6},{5,7},{6,4},{7,5},{8,10},{9,11},{10,... | collective-permute-start | bytes 442376 | tf_op jit(solution)/shard_map/ppermute | solution.py:811
  40.5 2.5 %collective-permute-start.10 = (bf16[96,768]{1,0:T(8,128)(2,1)S(1)}, bf16[96,768]{1,0:T(8,128)(2,1)S(1)}, u32[]{:S(2)}, u32[]{:S(2)}) collective-permute-start(bf16[96,768]{1,0:T(8,128)(2,1)S(1)} %collective-permute-done.6.refs_5_), channel_id=1, source_target_pairs={{0,2},{1,3},{2,0},{3,1},{4,6},{5,7},{6,4},{7,5},{8,10},{9,11},{10,... | collective-permute-start | bytes 442376 | tf_op jit(solution)/shard_map/ppermute | solution.py:811
  49.3 13.1 %collective-permute-start.12 = (bf16[512,384]{1,0:T(8,128)(2,1)}, bf16[512,384]{1,0:T(8,128)(2,1)S(1)}, u32[]{:S(2)}, u32[]{:S(2)}) collective-permute-start(bf16[512,384]{1,0:T(8,128)(2,1)} %get-tuple-element.84.refs_0_), channel_id=1, source_target_pairs={{0,4},{1,5},{2,3},{3,2},{4,0},{5,1},{6,7},{7,6},{8,12},{9,13},{10,... | collective-permute-start | bytes 1179656 | tf_op jit(solution)/shard_map/ppermute | solution.py:811
  50.1 14.6 %collective-permute-start.13 = (bf16[512,384]{1,0:T(8,128)(2,1)}, bf16[512,384]{1,0:T(8,128)(2,1)S(1)}, u32[]{:S(2)}, u32[]{:S(2)}) collective-permute-start(bf16[512,384]{1,0:T(8,128)(2,1)} %get-tuple-element.84.refs_0_), channel_id=1, source_target_pairs={{0,1},{1,0},{2,6},{3,7},{4,5},{5,4},{6,2},{7,3},{8,9},{9,8},{10,14... | collective-permute-start | bytes 1179656 | tf_op jit(solution)/shard_map/ppermute | solution.py:811
  62.4 9.7 %collective-permute-start.14 = (bf16[512,384]{1,0:T(8,128)(2,1)S(1)}, bf16[512,384]{1,0:T(8,128)(2,1)S(1)}, u32[]{:S(2)}, u32[]{:S(2)}) collective-permute-start(bf16[512,384]{1,0:T(8,128)(2,1)S(1)} %collective-permute-done.12.refs_1_), channel_id=1, source_target_pairs={{0,1},{1,0},{2,6},{3,7},{4,5},{5,4},{6,2},{7,3},{8,9},{9,8},{10,14... | collective-permute-start | bytes 1179656 | tf_op jit(solution)/shard_map/ppermute | solution.py:811
  64.2 7.9 %collective-permute-start.15 = (bf16[512,384]{1,0:T(8,128)(2,1)}, bf16[512,384]{1,0:T(8,128)(2,1)S(1)}, u32[]{:S(2)}, u32[]{:S(2)}) collective-permute-start(bf16[512,384]{1,0:T(8,128)(2,1)} %get-tuple-element.84.refs_0_), channel_id=1, source_target_pairs={{0,2},{1,3},{2,0},{3,1},{4,6},{5,7},{6,4},{7,5},{8,10},{9,11},{10,... | collective-permute-start | bytes 1179656 | tf_op jit(solution)/shard_map/ppermute | solution.py:811
  64.2 8.0 %collective-permute-start.16 = (bf16[512,384]{1,0:T(8,128)(2,1)S(1)}, bf16[512,384]{1,0:T(8,128)(2,1)S(1)}, u32[]{:S(2)}, u32[]{:S(2)}) collective-permute-start(bf16[512,384]{1,0:T(8,128)(2,1)S(1)} %collective-permute-done.12.refs_1_), channel_id=1, source_target_pairs={{0,2},{1,3},{2,0},{3,1},{4,6},{5,7},{6,4},{7,5},{8,10},{9,11},{10,... | collective-permute-start | bytes 1179656 | tf_op jit(solution)/shard_map/ppermute | solution.py:811
  64.7 7.5 %collective-permute-start.17 = (bf16[512,384]{1,0:T(8,128)(2,1)S(1)}, bf16[512,384]{1,0:T(8,128)(2,1)S(1)}, u32[]{:S(2)}, u32[]{:S(2)}) collective-permute-start(bf16[512,384]{1,0:T(8,128)(2,1)S(1)} %collective-permute-done.13.refs_2_), channel_id=1, source_target_pairs={{0,2},{1,3},{2,0},{3,1},{4,6},{5,7},{6,4},{7,5},{8,10},{9,11},{10,... | collective-permute-start | bytes 1179656 | tf_op jit(solution)/shard_map/ppermute | solution.py:811
  89.5 18.4 %collective-permute-start.19 = (bf16[128,256]{1,0:T(8,128)(2,1)}, bf16[128,256]{1,0:T(8,128)(2,1)S(1)}, u32[]{:S(2)}, u32[]{:S(2)}) collective-permute-start(bf16[128,256]{1,0:T(8,128)(2,1)} %get-tuple-element.88), channel_id=1, source_target_pairs={{0,8},{1,9},{2,10},{3,11},{4,12},{5,13},{6,14},{7,15},{8,0},{9,1},... | collective-permute-start | bytes 196616 | tf_op jit(solution)/shard_map/ppermute | solution.py:811
  90.5 17.4 %collective-permute-start.20 = (bf16[128,256]{1,0:T(8,128)(2,1)}, bf16[128,256]{1,0:T(8,128)(2,1)S(1)}, u32[]{:S(2)}, u32[]{:S(2)}) collective-permute-start(bf16[128,256]{1,0:T(8,128)(2,1)} %get-tuple-element.89), channel_id=1, source_target_pairs={{0,16},{1,17},{2,18},{3,19},{4,20},{5,21},{6,22},{7,23},{8,24},{9,... | collective-permute-start | bytes 196616 | tf_op jit(solution)/shard_map/ppermute | solution.py:811
  92.2 15.8 %collective-permute-start.21 = (bf16[128,256]{1,0:T(8,128)(2,1)}, bf16[128,256]{1,0:T(8,128)(2,1)S(1)}, u32[]{:S(2)}, u32[]{:S(2)}) collective-permute-start(bf16[128,256]{1,0:T(8,128)(2,1)} %get-tuple-element.90), channel_id=1, source_target_pairs={{0,24},{1,25},{2,26},{3,27},{4,28},{5,29},{6,30},{7,31},{8,16},{9,... | collective-permute-start | bytes 196616 | tf_op jit(solution)/shard_map/ppermute | solution.py:811
  122.3 7.0 %collective-permute-start.22 = (bf16[96,256]{1,0:T(8,128)(2,1)}, bf16[96,256]{1,0:T(8,128)(2,1)S(1)}, u32[]{:S(2)}, u32[]{:S(2)}) collective-permute-start(bf16[96,256]{1,0:T(8,128)(2,1)} %get-tuple-element.118), channel_id=1, source_target_pairs={{0,8},{1,9},{2,10},{3,11},{4,12},{5,13},{6,14},{7,15},{8,0},{9,1},... | collective-permute-start | bytes 147464 | tf_op jit(solution)/shard_map/ppermute | solution.py:811
  122.3 7.9 %collective-permute-start.23 = (bf16[96,256]{1,0:T(8,128)(2,1)}, bf16[96,256]{1,0:T(8,128)(2,1)S(1)}, u32[]{:S(2)}, u32[]{:S(2)}) collective-permute-start(bf16[96,256]{1,0:T(8,128)(2,1)} %get-tuple-element.119), channel_id=1, source_target_pairs={{0,16},{1,17},{2,18},{3,19},{4,20},{5,21},{6,22},{7,23},{8,24},{9,... | collective-permute-start | bytes 147464 | tf_op jit(solution)/shard_map/ppermute | solution.py:811
  124.3 6.2 %collective-permute-start.24 = (bf16[96,256]{1,0:T(8,128)(2,1)}, bf16[96,256]{1,0:T(8,128)(2,1)S(1)}, u32[]{:S(2)}, u32[]{:S(2)}) collective-permute-start(bf16[96,256]{1,0:T(8,128)(2,1)} %get-tuple-element.120), channel_id=1, source_target_pairs={{0,24},{1,25},{2,26},{3,27},{4,28},{5,29},{6,30},{7,31},{8,16},{9,... | collective-permute-start | bytes 147464 | tf_op jit(solution)/shard_map/ppermute | solution.py:811
  126.7 19.7 %collective-permute-start.27 = (bf16[512,256]{1,0:T(8,128)(2,1)S(1)}, bf16[512,256]{1,0:T(8,128)(2,1)S(1)}, u32[]{:S(2)}, u32[]{:S(2)}) collective-permute-start(bf16[512,256]{1,0:T(8,128)(2,1)S(1)} %copy-done.2), channel_id=1, source_target_pairs={{0,4},{1,5},{2,3},{3,2},{4,0},{5,1},{6,7},{7,6},{8,12},{9,13},{10,... | collective-permute-start | bytes 786440 | tf_op jit(solution)/shard_map/ppermute | solution.py:811
  127.8 18.8 %collective-permute-start.28 = (bf16[512,256]{1,0:T(8,128)(2,1)S(1)}, bf16[512,256]{1,0:T(8,128)(2,1)S(1)}, u32[]{:S(2)}, u32[]{:S(2)}) collective-permute-start(bf16[512,256]{1,0:T(8,128)(2,1)S(1)} %copy-done.2), channel_id=1, source_target_pairs={{0,1},{1,0},{2,6},{3,7},{4,5},{5,4},{6,2},{7,3},{8,9},{9,8},{10,14... | collective-permute-start | bytes 786440 | tf_op jit(solution)/shard_map/ppermute | solution.py:811
  129.2 19.4 %collective-permute-start.29 = (bf16[512,256]{1,0:T(8,128)(2,1)S(1)}, bf16[512,256]{1,0:T(8,128)(2,1)S(1)}, u32[]{:S(2)}, u32[]{:S(2)}) collective-permute-start(bf16[512,256]{1,0:T(8,128)(2,1)S(1)} %copy-done.2), channel_id=1, source_target_pairs={{0,5},{1,4},{2,7},{3,6},{4,1},{5,0},{6,3},{7,2},{8,13},{9,12},{10,... | collective-permute-start | bytes 786440 | tf_op jit(solution)/shard_map/ppermute | solution.py:811
  133.8 13.3 %collective-permute-start.25 = (bf16[512,256]{1,0:T(8,128)(2,1)}, bf16[512,256]{1,0:T(8,128)(2,1)S(1)}, u32[]{:S(2)}, u32[]{:S(2)}) collective-permute-start(bf16[512,256]{1,0:T(8,128)(2,1)} %delta.1.g_ref.refs_11_), channel_id=1, source_target_pairs={{0,4},{1,5},{2,3},{3,2},{4,0},{5,1},{6,7},{7,6},{8,12},{9,13},{10,... | collective-permute-start | bytes 786440 | tf_op jit(solution)/shard_map/ppermute | solution.py:811
  135.2 12.0 %collective-permute-start.26 = (bf16[512,256]{1,0:T(8,128)(2,1)}, bf16[512,256]{1,0:T(8,128)(2,1)S(1)}, u32[]{:S(2)}, u32[]{:S(2)}) collective-permute-start(bf16[512,256]{1,0:T(8,128)(2,1)} %delta.1.g_ref.refs_11_), channel_id=1, source_target_pairs={{0,1},{1,0},{2,6},{3,7},{4,5},{5,4},{6,2},{7,3},{8,9},{9,8},{10,14... | collective-permute-start | bytes 786440 | tf_op jit(solution)/shard_map/ppermute | solution.py:811
  146.6 2.6 %collective-permute-start.31 = (bf16[512,256]{1,0:T(8,128)(2,1)S(1)}, bf16[512,256]{1,0:T(8,128)(2,1)S(1)}, u32[]{:S(2)}, u32[]{:S(2)}) collective-permute-start(bf16[512,256]{1,0:T(8,128)(2,1)S(1)} %collective-permute-done.27.refs_4_), channel_id=1, source_target_pairs={{0,2},{1,3},{2,0},{3,1},{4,6},{5,7},{6,4},{7,5},{8,10},{9,11},{10,... | collective-permute-start | bytes 786440 | tf_op jit(solution)/shard_map/ppermute | solution.py:811
  147.2 6.4 %collective-permute-start.34 = (bf16[512,256]{1,0:T(8,128)(2,1)S(1)}, bf16[512,256]{1,0:T(8,128)(2,1)S(1)}, u32[]{:S(2)}, u32[]{:S(2)}) collective-permute-start(bf16[512,256]{1,0:T(8,128)(2,1)S(1)} %collective-permute-done.25.refs_12_), channel_id=1, source_target_pairs={{0,1},{1,0},{2,6},{3,7},{4,5},{5,4},{6,2},{7,3},{8,9},{9,8},{10,14... | collective-permute-start | bytes 786440 | tf_op jit(solution)/shard_map/ppermute | solution.py:811
  148.6 5.0 %collective-permute-start.33 = (bf16[512,256]{1,0:T(8,128)(2,1)S(1)}, bf16[512,256]{1,0:T(8,128)(2,1)S(1)}, u32[]{:S(2)}, u32[]{:S(2)}) collective-permute-start(bf16[512,256]{1,0:T(8,128)(2,1)S(1)} %collective-permute-done.29.refs_6_), channel_id=1, source_target_pairs={{0,2},{1,3},{2,0},{3,1},{4,6},{5,7},{6,4},{7,5},{8,10},{9,11},{10,... | collective-permute-start | bytes 786440 | tf_op jit(solution)/shard_map/ppermute | solution.py:811
  148.7 5.0 %collective-permute-start.36 = (bf16[512,256]{1,0:T(8,128)(2,1)S(1)}, bf16[512,256]{1,0:T(8,128)(2,1)S(1)}, u32[]{:S(2)}, u32[]{:S(2)}) collective-permute-start(bf16[512,256]{1,0:T(8,128)(2,1)S(1)} %collective-permute-done.25.refs_12_), channel_id=1, source_target_pairs={{0,2},{1,3},{2,0},{3,1},{4,6},{5,7},{6,4},{7,5},{8,10},{9,11},{10,... | collective-permute-start | bytes 786440 | tf_op jit(solution)/shard_map/ppermute | solution.py:811
  149.2 4.5 %collective-permute-start.35 = (bf16[512,256]{1,0:T(8,128)(2,1)S(1)}, bf16[512,256]{1,0:T(8,128)(2,1)S(1)}, u32[]{:S(2)}, u32[]{:S(2)}) collective-permute-start(bf16[512,256]{1,0:T(8,128)(2,1)S(1)} %copy-done.4), channel_id=1, source_target_pairs={{0,2},{1,3},{2,0},{3,1},{4,6},{5,7},{6,4},{7,5},{8,10},{9,11},{10,... | collective-permute-start | bytes 786440 | tf_op jit(solution)/shard_map/ppermute | solution.py:811
  149.3 4.4 %collective-permute-start.37 = (bf16[512,256]{1,0:T(8,128)(2,1)S(1)}, bf16[512,256]{1,0:T(8,128)(2,1)S(1)}, u32[]{:S(2)}, u32[]{:S(2)}) collective-permute-start(bf16[512,256]{1,0:T(8,128)(2,1)S(1)} %collective-permute-done.26.refs_13_), channel_id=1, source_target_pairs={{0,2},{1,3},{2,0},{3,1},{4,6},{5,7},{6,4},{7,5},{8,10},{9,11},{10,... | collective-permute-start | bytes 786440 | tf_op jit(solution)/shard_map/ppermute | solution.py:811
  177.2 13.6 %collective-permute-start.39 = (bf16[256,768]{1,0:T(8,128)(2,1)}, bf16[256,768]{1,0:T(8,128)(2,1)S(1)}, u32[]{:S(2)}, u32[]{:S(2)}) collective-permute-start(bf16[256,768]{1,0:T(8,128)(2,1)} %get-tuple-element.133), channel_id=1, source_target_pairs={{0,8},{1,9},{2,10},{3,11},{4,12},{5,13},{6,14},{7,15},{8,0},{9,1},... | collective-permute-start | bytes 1179656 | tf_op jit(solution)/shard_map/ppermute | solution.py:811
  180.0 5.7 %collective-permute-start.44 = (bf16[40,768]{1,0:T(8,128)(2,1)S(1)}, bf16[40,768]{1,0:T(8,128)(2,1)S(1)}, u32[]{:S(2)}, u32[]{:S(2)}) collective-permute-start(bf16[40,768]{1,0:T(8,128)(2,1)S(1)} %get-tuple-element.151), channel_id=1, source_target_pairs={{0,5},{1,4},{2,7},{3,6},{4,1},{5,0},{6,3},{7,2},{8,13},{9,12},{10,... | collective-permute-start | bytes 184328 | tf_op jit(solution)/shard_map/ppermute | solution.py:811
  180.1 5.6 %collective-permute-start.43 = (bf16[40,768]{1,0:T(8,128)(2,1)S(1)}, bf16[40,768]{1,0:T(8,128)(2,1)S(1)}, u32[]{:S(2)}, u32[]{:S(2)}) collective-permute-start(bf16[40,768]{1,0:T(8,128)(2,1)S(1)} %get-tuple-element.152), channel_id=1, source_target_pairs={{0,4},{1,5},{2,6},{3,7},{4,0},{5,1},{6,2},{7,3},{8,12},{9,13},{10,... | collective-permute-start | bytes 184328 | tf_op jit(solution)/shard_map/ppermute | solution.py:811
  180.1 6.2 %collective-permute-start.42 = (bf16[40,768]{1,0:T(8,128)(2,1)S(1)}, bf16[40,768]{1,0:T(8,128)(2,1)S(1)}, u32[]{:S(2)}, u32[]{:S(2)}) collective-permute-start(bf16[40,768]{1,0:T(8,128)(2,1)S(1)} %get-tuple-element.150), channel_id=1, source_target_pairs={{0,1},{1,0},{2,3},{3,2},{4,5},{5,4},{6,7},{7,6},{8,9},{9,8},{10,11... | collective-permute-start | bytes 184328 | tf_op jit(solution)/shard_map/ppermute | solution.py:811
  186.4 6.2 %collective-permute-start.47 = (bf16[40,768]{1,0:T(8,128)(2,1)S(1)}, bf16[40,768]{1,0:T(8,128)(2,1)S(1)}, u32[]{:S(2)}, u32[]{:S(2)}) collective-permute-start(bf16[40,768]{1,0:T(8,128)(2,1)S(1)} %fusion.3), channel_id=1, source_target_pairs={{0,24},{1,25},{2,26},{3,27},{4,28},{5,29},{6,30},{7,31},{8,16},{9,... | collective-permute-start | bytes 184328 | tf_op jit(solution)/shard_map/ppermute | solution.py:811
  188.6 10.3 %collective-permute-start.46 = (bf16[40,768]{1,0:T(8,128)(2,1)S(1)}, bf16[40,768]{1,0:T(8,128)(2,1)S(1)}, u32[]{:S(2)}, u32[]{:S(2)}) collective-permute-start(bf16[40,768]{1,0:T(8,128)(2,1)S(1)} %fusion.3), channel_id=1, source_target_pairs={{0,16},{1,17},{2,18},{3,19},{4,20},{5,21},{6,22},{7,23},{8,24},{9,... | collective-permute-start | bytes 184328 | tf_op jit(solution)/shard_map/ppermute | solution.py:811
  188.6 10.3 %collective-permute-start.45 = (bf16[40,768]{1,0:T(8,128)(2,1)S(1)}, bf16[40,768]{1,0:T(8,128)(2,1)S(1)}, u32[]{:S(2)}, u32[]{:S(2)}) collective-permute-start(bf16[40,768]{1,0:T(8,128)(2,1)S(1)} %fusion.3), channel_id=1, source_target_pairs={{0,8},{1,9},{2,10},{3,11},{4,12},{5,13},{6,14},{7,15},{8,0},{9,1},... | collective-permute-start | bytes 184328 | tf_op jit(solution)/shard_map/ppermute | solution.py:811
  190.9 19.3 %collective-permute-start.40 = (bf16[128,768]{1,0:T(8,128)(2,1)S(1)}, bf16[128,768]{1,0:T(8,128)(2,1)S(1)}, u32[]{:S(2)}, u32[]{:S(2)}) collective-permute-start(bf16[128,768]{1,0:T(8,128)(2,1)S(1)} %slice.48), channel_id=1, source_target_pairs={{0,16},{1,17},{2,18},{3,19},{4,20},{5,21},{6,22},{7,23},{8,24},{9,... | collective-permute-start | bytes 589832 | tf_op jit(solution)/shard_map/ppermute | solution.py:811
  198.9 4.3 %collective-permute-start.48 = (bf16[40,768]{1,0:T(8,128)(2,1)S(1)}, bf16[40,768]{1,0:T(8,128)(2,1)S(1)}, u32[]{:S(2)}, u32[]{:S(2)}) collective-permute-start(bf16[40,768]{1,0:T(8,128)(2,1)S(1)} %add_convert_fusion.refs_0_), channel_id=1, source_target_pairs={{0,1},{1,0},{2,3},{3,2},{4,5},{5,4},{6,7},{7,6},{8,9},{9,8},{10,11... | collective-permute-start | bytes 184328 | tf_op jit(solution)/shard_map/ppermute | solution.py:811
  200.9 4.2 %collective-permute-start.49 = (bf16[40,768]{1,0:T(8,128)(2,1)S(1)}, bf16[40,768]{1,0:T(8,128)(2,1)S(1)}, u32[]{:S(2)}, u32[]{:S(2)}) collective-permute-start(bf16[40,768]{1,0:T(8,128)(2,1)S(1)} %add_convert_fusion.refs_0_), channel_id=1, source_target_pairs={{0,4},{1,5},{2,6},{3,7},{4,0},{5,1},{6,2},{7,3},{8,12},{9,13},{10,... | collective-permute-start | bytes 184328 | tf_op jit(solution)/shard_map/ppermute | solution.py:811
  200.9 5.1 %collective-permute-start.50 = (bf16[40,768]{1,0:T(8,128)(2,1)S(1)}, bf16[40,768]{1,0:T(8,128)(2,1)S(1)}, u32[]{:S(2)}, u32[]{:S(2)}) collective-permute-start(bf16[40,768]{1,0:T(8,128)(2,1)S(1)} %add_convert_fusion.refs_0_), channel_id=1, source_target_pairs={{0,5},{1,4},{2,7},{3,6},{4,1},{5,0},{6,3},{7,2},{8,13},{9,12},{10,... | collective-permute-start | bytes 184328 | tf_op jit(solution)/shard_map/ppermute | solution.py:811
  202.5 3.6 %collective-permute-start.51 = (bf16[40,768]{1,0:T(8,128)(2,1)S(1)}, bf16[40,768]{1,0:T(8,128)(2,1)S(1)}, u32[]{:S(2)}, u32[]{:S(2)}) collective-permute-start(bf16[40,768]{1,0:T(8,128)(2,1)S(1)} %add_convert_fusion.refs_0_), channel_id=1, source_target_pairs={{0,2},{1,3},{2,0},{3,1},{4,6},{5,7},{6,4},{7,5},{8,10},{9,11},{10,... | collective-permute-start | bytes 184328 | tf_op jit(solution)/shard_map/ppermute | solution.py:811
  203.2 2.9 %collective-permute-start.52 = (bf16[40,768]{1,0:T(8,128)(2,1)S(1)}, bf16[40,768]{1,0:T(8,128)(2,1)S(1)}, u32[]{:S(2)}, u32[]{:S(2)}) collective-permute-start(bf16[40,768]{1,0:T(8,128)(2,1)S(1)} %collective-permute-done.48.refs_1_), channel_id=1, source_target_pairs={{0,2},{1,3},{2,0},{3,1},{4,6},{5,7},{6,4},{7,5},{8,10},{9,11},{10,... | collective-permute-start | bytes 184328 | tf_op jit(solution)/shard_map/ppermute | solution.py:811
  (62 other events, 350.5 us)
Sparse Core Ops, SparseCore 0:
  10.9 96.9 all-gather.1
